TPU v7x, 32 devices: a whole 2x2x4 slice. The times are simulated.
32 devices in a mesh: dp: 8 (over z, y), head: 4 (over x, core).
Axes of the slice: x: 2, y: 2, z: 4, core: 2. Of those that a mesh axis runs over, the one named last changes fastest.
Arguments:
- inputs: bfloat16 [56, 512, 768], P('dp', 'head'), may hold values from -6 to 6
- lengths: int32 [56], P('dp'), may hold values from 16 to 512, as said below
- query_weight: bfloat16 [768, 768], P(None, 'head'), may hold values from -0.21875 to 0.21875
- query_bias: bfloat16 [768], P('head'), may hold values from -3 to 3
- key_weight: bfloat16 [768, 768], P(None, 'head'), may hold values from -0.21875 to 0.21875
- value_weight: bfloat16 [768, 768], P(None, 'head'), may hold values from -0.21875 to 0.21875
- value_bias: bfloat16 [768], P('head'), may hold values from -1.1953125 to 1.1953125
- attention_out_weight: bfloat16 [768, 768], replicated, may hold values from -1.75 to 1.75
- output_bias: bfloat16 [768], replicated, may hold values from -3 to 3
- first_gain: bfloat16 [768], replicated, may hold values from 0.5 to 1.5
- first_shift: bfloat16 [768], replicated, may hold values from -3 to 3
- expand_weight: bfloat16 [768, 3072], replicated, may hold values from -0.21875 to 0.21875
- inner_bias: bfloat16 [3072], replicated, may hold values from -3 to 3
- contract_weight: bfloat16 [3072, 768], replicated, may hold values from -0.109375 to 0.109375
- outer_bias: bfloat16 [768], replicated, may hold values from -3 to 3
- second_gain: bfloat16 [768], replicated, may hold values from 0.5 to 1.5
- second_shift: bfloat16 [768], replicated, may hold values from -3 to 3
- cotangent: bfloat16 [56, 512, 768], P('dp', 'head'), may hold values from -6 to 6
Outputs:
- output: bfloat16 [56, 512, 768], P('dp', 'head')
- input_gradient: float32 [56, 512, 768], P('dp', 'head')
- query_weight_gradient: float32 [768, 768], P('dp', 'head')
- query_bias_gradient: float32 [768], replicated
- key_weight_gradient: float32 [768, 768], P('dp', 'head')
- value_weight_gradient: float32 [768, 768], P('dp', 'head')
- value_bias_gradient: float32 [768], replicated
- output_weight_gradient: float32 [768, 768], P(None, ('dp', 'head'))
- output_bias_gradient: float32 [768], replicated
- first_gain_gradient: float32 [768], replicated
- first_shift_gradient: float32 [768], replicated
- inner_weight_gradient: float32 [768, 3072], P(None, ('dp', 'head'))
- inner_bias_gradient: float32 [3072], replicated
- outer_weight_gradient: float32 [3072, 768], P(('dp', 'head'))
- outer_bias_gradient: float32 [768], replicated
- second_gain_gradient: float32 [768], replicated
- second_shift_gradient: float32 [768], replicated
Inputs may be any that keep to these rules, and one draw needn't show every extreme that they name: `lengths`: in each aligned block of 7 sequences, one has length exactly 512.
All inputs are finite; a program needn't handle non-finite values.
Results may differ from a plain program's by a relative error of at most 0.015.
Values may be sent and summed in bfloat16 or wider, within the bound.
A program may use at most 192 MiB of HBM per device.

v0:
```python
import jax
import jax.numpy as jnp
from jax import lax
from jax.sharding import PartitionSpec as P

HEAD_DIM = 64


EPSILON = 1e-12
MASKED = -1e30
SCALE = 0.125


def normalize(hidden, gain, shift):
    center = hidden - jnp.mean(hidden, axis=-1, keepdims=True)
    inverse = lax.rsqrt(jnp.mean(center * center, axis=-1, keepdims=True) + EPSILON)
    normed = center * inverse
    return (normed * gain + shift, normed, inverse)


def normalize_back(upstream, normed, inverse, gain):
    scaled = upstream * gain
    inner_term = (
        scaled
        - jnp.mean(scaled, axis=-1, keepdims=True)
        - normed * jnp.mean(scaled * normed, axis=-1, keepdims=True)
    )
    return inverse * inner_term


def gelu_slope(hidden_in):
    cumulative = 0.5 * (1.0 + lax.erf(hidden_in * 0.7071067811865476))
    return cumulative + hidden_in * jnp.exp(-0.5 * hidden_in * hidden_in) * 0.3989422804014327


def masked_scores(queries, key_rows, visible):
    raw_scores = (
        jnp.einsum("qhd,khd->hqk", queries, key_rows, preferred_element_type=jnp.float32) * SCALE
    )
    return jnp.where(visible[None, None, :], raw_scores, MASKED)


def attend(block_items):
    queries, key_rows, values, visible = block_items
    scores = masked_scores(queries, key_rows, visible)
    row_max = jnp.max(scores, axis=-1, keepdims=True)
    exponent = jnp.exp(scores - row_max)
    row_total = jnp.sum(exponent, axis=-1, keepdims=True)
    weights = (exponent / row_total).astype(jnp.bfloat16)
    context = jnp.einsum("hqk,khd->qhd", weights, values, preferred_element_type=jnp.float32)
    return (context.astype(jnp.bfloat16), row_max + jnp.log(row_total))


def attend_back(block_items):
    queries, key_rows, values, visible, upstream, logsum = block_items
    scores = masked_scores(queries, key_rows, visible)
    probabilities = jnp.exp(scores - logsum)
    weights = probabilities.astype(jnp.bfloat16)
    dprobs = jnp.einsum("qhd,khd->hqk", upstream, values, preferred_element_type=jnp.float32)
    row_delta = jnp.sum(probabilities * dprobs, axis=-1, keepdims=True)
    dscores = (probabilities * (dprobs - row_delta)).astype(jnp.bfloat16)
    dvalues = jnp.einsum(
        "hqk,qhd->khd", weights, upstream, preferred_element_type=jnp.float32
    ).astype(jnp.bfloat16)
    dqueries = (
        jnp.einsum("hqk,khd->qhd", dscores, key_rows, preferred_element_type=jnp.float32) * SCALE
    ).astype(jnp.bfloat16)
    dkeys = (
        jnp.einsum("hqk,qhd->khd", dscores, queries, preferred_element_type=jnp.float32) * SCALE
    ).astype(jnp.bfloat16)
    return (dqueries, dkeys, dvalues)


def on_device(
    inputs,
    lengths,
    query_weight,
    query_bias,
    key_weight,
    value_weight,
    value_bias,
    attention_out_weight,
    output_bias,
    first_gain,
    first_shift,
    expand_weight,
    inner_bias,
    contract_weight,
    outer_bias,
    second_gain,
    second_shift,
    cotangent,
):
    groups = inputs.shape[0]
    model_width = inputs.shape[2]
    local_width = query_weight.shape[1]
    heads_local = local_width // HEAD_DIM
    gathered_rows = lax.all_gather(inputs, "head", axis=1, tiled=True)
    full_length = gathered_rows.shape[1]
    combined_weight = jnp.concatenate([query_weight, key_weight, value_weight], axis=1)
    projected = jnp.einsum(
        "bhj,ja->bha", gathered_rows, combined_weight, preferred_element_type=jnp.float32
    )
    head_dims = (groups, full_length, heads_local, HEAD_DIM)
    queries = (
        (projected[..., :local_width] + query_bias.astype(jnp.float32))
        .astype(jnp.bfloat16)
        .reshape(head_dims)
    )
    key_rows = projected[..., local_width : 2 * local_width].astype(jnp.bfloat16).reshape(head_dims)
    values = (
        (projected[..., 2 * local_width :] + value_bias.astype(jnp.float32))
        .astype(jnp.bfloat16)
        .reshape(head_dims)
    )
    visible = jnp.arange(full_length, dtype=jnp.int32)[None, :] < lengths[:, None]
    context, logsum = lax.map(attend, (queries, key_rows, values, visible))
    context = context.reshape(groups, full_length, local_width)
    context_token_rows = lax.all_to_all(context, "head", split_axis=1, concat_axis=2, tiled=True)
    residual = inputs.astype(jnp.float32)
    attended = jnp.einsum(
        "bhj,ja->bha", context_token_rows, attention_out_weight, preferred_element_type=jnp.float32
    ) + output_bias.astype(jnp.float32)
    first_gain_f = first_gain.astype(jnp.float32)
    second_gain_f = second_gain.astype(jnp.float32)
    first_out, first_normed, first_inverse = normalize(
        residual + attended, first_gain_f, first_shift.astype(jnp.float32)
    )
    first_lower_part = first_out.astype(jnp.bfloat16)
    hidden_in = jnp.einsum(
        "bhj,ja->bha", first_lower_part, expand_weight, preferred_element_type=jnp.float32
    ) + inner_bias.astype(jnp.float32)
    active_lower_part = jax.nn.gelu(hidden_in, approximate=False).astype(jnp.bfloat16)
    branch = jnp.einsum(
        "wfy,yu->wfu", active_lower_part, contract_weight, preferred_element_type=jnp.float32
    ) + outer_bias.astype(jnp.float32)
    normed_out, second_normed, second_inverse = normalize(
        first_out + branch, second_gain_f, second_shift.astype(jnp.float32)
    )
    output = normed_out.astype(jnp.bfloat16)
    upstream = cotangent.astype(jnp.float32)
    second_gain_grad = jnp.sum(upstream * second_normed, axis=(0, 1))
    second_shift_grad = jnp.sum(upstream, axis=(0, 1))
    dsecond = normalize_back(upstream, second_normed, second_inverse, second_gain_f)
    branch_gradient = dsecond.astype(jnp.bfloat16)
    outer_bias_grad = jnp.sum(branch_gradient.astype(jnp.float32), axis=(0, 1))
    outer_weight_grad = jnp.einsum(
        "zrp,zrx->px", active_lower_part, branch_gradient, preferred_element_type=jnp.float32
    )
    active_gradient = jnp.einsum(
        "ofv,jv->ofj", branch_gradient, contract_weight, preferred_element_type=jnp.float32
    )
    hidden_gradient = (active_gradient * gelu_slope(hidden_in)).astype(jnp.bfloat16)
    inner_bias_grad = jnp.sum(hidden_gradient.astype(jnp.float32), axis=(0, 1))
    inner_weight_grad = jnp.einsum(
        "vrb,vrm->bm", first_lower_part, hidden_gradient, preferred_element_type=jnp.float32
    )
    dfirst = (
        jnp.einsum(
            "hiy,qy->hiq", hidden_gradient, expand_weight, preferred_element_type=jnp.float32
        )
        + dsecond
    )
    first_gain_grad = jnp.sum(dfirst * first_normed, axis=(0, 1))
    first_shift_grad = jnp.sum(dfirst, axis=(0, 1))
    dsum = normalize_back(dfirst, first_normed, first_inverse, first_gain_f)
    attended_gradient = dsum.astype(jnp.bfloat16)
    output_bias_grad = jnp.sum(attended_gradient.astype(jnp.float32), axis=(0, 1))
    output_weight_grad = jnp.einsum(
        "zrp,zrx->px", context_token_rows, attended_gradient, preferred_element_type=jnp.float32
    )
    dcontext = jnp.einsum(
        "ofv,jv->ofj", attended_gradient, attention_out_weight, preferred_element_type=jnp.float32
    ).astype(jnp.bfloat16)
    dcontext_heads = lax.all_to_all(
        dcontext, "head", split_axis=2, concat_axis=1, tiled=True
    ).reshape(head_dims)
    dqueries, dkeys, dvalues = lax.map(
        attend_back, (queries, key_rows, values, visible, dcontext_heads, logsum)
    )
    flat_dims = (groups, full_length, local_width)
    joint_gradient = jnp.concatenate(
        [dqueries.reshape(flat_dims), dkeys.reshape(flat_dims), dvalues.reshape(flat_dims)], axis=2
    )
    query_bias_grad = jnp.sum(dqueries.reshape(flat_dims).astype(jnp.float32), axis=(0, 1))
    value_bias_grad = jnp.sum(dvalues.reshape(flat_dims).astype(jnp.float32), axis=(0, 1))
    source_token_rows = lax.all_gather(inputs, "head", axis=1, tiled=True)
    combined_gradient = jnp.einsum(
        "vrb,vrm->bm", source_token_rows, joint_gradient, preferred_element_type=jnp.float32
    )
    partial_gradient = jnp.einsum(
        "hiy,qy->hiq", joint_gradient, combined_weight, preferred_element_type=jnp.float32
    )
    input_gradient = (
        lax.psum_scatter(
            partial_gradient.astype(jnp.bfloat16), "head", scatter_dimension=1, tiled=True
        ).astype(jnp.float32)
        + dsum
    )
    head_index = lax.axis_index("head")
    zeros_width = jnp.zeros((model_width,), jnp.float32)
    query_bias_full = lax.dynamic_update_slice_in_dim(
        zeros_width, query_bias_grad, head_index * local_width, 0
    )
    value_bias_full = lax.dynamic_update_slice_in_dim(
        zeros_width, value_bias_grad, head_index * local_width, 0
    )
    head_part = lax.psum_scatter(combined_gradient, "dp", scatter_dimension=0, tiled=True)
    small_sums = lax.psum(
        (
            query_bias_full,
            value_bias_full,
            output_bias_grad,
            first_gain_grad,
            first_shift_grad,
            inner_bias_grad,
            outer_bias_grad,
            second_gain_grad,
            second_shift_grad,
        ),
        ("dp", "head"),
    )
    shared = (
        lax.psum_scatter(output_weight_grad, ("dp", "head"), scatter_dimension=1, tiled=True),
        lax.psum_scatter(inner_weight_grad, ("dp", "head"), scatter_dimension=1, tiled=True),
        lax.psum_scatter(outer_weight_grad, ("dp", "head"), scatter_dimension=0, tiled=True),
    )
    return (
        output,
        input_gradient,
        head_part[:, :local_width],
        small_sums[0],
        head_part[:, local_width : 2 * local_width],
        head_part[:, 2 * local_width :],
        small_sums[1],
        shared[0],
        small_sums[2],
        small_sums[3],
        small_sums[4],
        shared[1],
        small_sums[5],
        shared[2],
        small_sums[6],
        small_sums[7],
        small_sums[8],
    )


def solution(mesh):
    in_specs = (
        P("dp", "head", None),
        P("dp"),
        P(None, "head"),
        P("head"),
        P(None, "head"),
        P(None, "head"),
        P("head"),
        P(),
        P(),
        P(),
        P(),
        P(),
        P(),
        P(),
        P(),
        P(),
        P(),
        P("dp", "head", None),
    )
    out_specs = (
        P("dp", "head", None),
        P("dp", "head", None),
        P("dp", "head"),
        P(),
        P("dp", "head"),
        P("dp", "head"),
        P(),
        P(None, ("dp", "head")),
        P(),
        P(),
        P(),
        P(None, ("dp", "head")),
        P(),
        P(("dp", "head"), None),
        P(),
        P(),
        P(),
    )
    return jax.shard_map(
        on_device, mesh=mesh, in_specs=in_specs, out_specs=out_specs, check_vma=False
    )
```

profile of v0, /device:TPU:0, one launch (start us, length us, event | category | flops | bytes accessed | tf_op | source)
XLA Modules:
  0.0 851.0 jit_solution(7159350012995066577)
XLA Ops:
  10.0 44.3 %all-gather.2.cloned.1.call-done = bf16[7,512,768]{2,1,0:T(8,128)(2,1)} async-done(((bf16[7,128,768]{2,1,0:T(8,128)(2,1)}), bf16[7,512,768]{2,1,0:T(8,128)(2,1)}) %all-gather.2.cloned.1.call-update) | async-done | bytes 5505040 | tf_op jit(solution)/shard_map/all_gather | solution.py:98
  54.3 5.8 convolution_bitcast_fusion.2
  63.9 35.1 %while.26 = (s32[]{:T(128)}, bf16[7,512,3,64]{1,3,2,0:T(8,128)(2,1)}, f32[7,3,512,1]{2,1,3,0:T(4,128)S(1)}, bf16[7,512,3,64]{1,3,2,0:T(8,128)(2,1)}, pred[7,512]...) while((s32[]{:T(128)}, ...), condition=%wide.region_3.4_spmd, body=%wide.region_0.3_spmd.sunk | while | flops 210860544 | bytes 10283613 | solution.py:117
  66.4 2.6 fusion.142
  71.4 2.6 fusion.142
  99.0 4.3 copy.97
  103.4 5.1 all-to-all-start
  108.6 25.6 %all-to-all-done = bf16[7,512,192]{2,0,1:T(8,128)(2,1)} async-done(((bf16[7,512,192]{2,0,1:T(8,128)(2,1)}), bf16[7,512,192]{2,0,1:T(8,128)(2,1)}, u32[]{:S(2)}, u32[]{:S(2)}) %all-to-all-start) | async-done | bytes 1376288 | tf_op jit(solution)/shard_map/all_to_all | solution.py:119
  134.2 3.5 copy.120
  141.6 11.0 %fusion.86 = (u8[128,3072]{1,0:T(8,128)(4,1)S(1)}, u8[128,3072]{1,0:T(8,128)(4,1)S(1)}, f32[7,128,3072]{2,1,0:T(8,128)S(1)}) fusion(f32[3072]{0:T(1024)S(1)} %convert_element_type.126, bf16[768,3072]{1,0:T(8,128)(2,1)} %param.33, f32[7,128,768]{2,1,0:T(8,128)S(1)} %get-tuple-element.267, f32[768]{0:T(1024)S(1)} %convert_element_type.124, ...), kind=kOutput, calls=%fused_computation.132 | convolution fusion | flops 4269047808 | bytes 19293184 | tf_op jit(solution)/shard_map/bhj,ja->bha/dot_general | solution.py:130
  152.6 25.6 %fusion.56 = bf16[7,128,3072]{2,1,0:T(8,128)(2,1)S(1)} fusion(f32[7,128,3072]{2,1,0:T(8,128)S(1)} %get-tuple-element.268, f32[3072]{0:T(1024)S(1)} %convert_element_type.126, u8[128,3072]{1,0:T(8,128)(4,1)S(1)} %get-tuple-element.200, u8[128,3072]{1,0:T(8,128)(4,1)S(1)} %get-tuple-element.199), kind=kLoop, calls=%fused_computation.64 | loop fusion | flops 195428352 | bytes 17313792 | tf_op jit(solution)/shard_map/convert_element_type | solution.py:133
  178.2 4.8 fusion.108
  187.9 10.8 %convert_reduce_fusion = (f32[3072]{0:T(1024)S(1)}, bf16[7,128,3072]{2,1,0:T(8,128)(2,1)}) fusion(f32[7,128,3072]{2,1,0:T(8,128)S(1)} %get-tuple-element.268, f32[3072]{0:T(1024)S(1)} %convert_element_type.126, bf16[7,128,768]{2,1,0:T(8,128)(2,1)S(1)} %get-tuple-element.253, bf16[3072,768]{1,0:T(8,128)(2,1)S(1)} %bitcast.185), kind=kOutput, calls=%fused_computation.76 | convolution fusion | flops 4263638016 | bytes 22634496 | tf_op jit(solution)/shard_map/ofv,jv->ofj/dot_general | solution.py:150
  198.8 9.5 %multiply_reduce_fusion.1 = (f32[768]{0:T(1024)S(1)}, f32[7,128]{1,0:T(8,128)S(1)}, f32[7,128]{1,0:T(8,128)S(1)}, f32[768]{0:T(1024)S(1)}, f32[7,128,768]{2,1,0:T(8,128)S(1)}) fusion(f32[7,128,768]{2,1,0:T(8,128)S(1)} %get-tuple-element.267, f32[7,128]{1,0:T(8,128)S(1)} %add_rsqrt_fusion.1, f32[7,128]{1,0:T(8,128)S(1)} %broadcast_multiply_fusion.5, ...), kind=kOutput, calls=%fused_computation.118 | convolution fusion | flops 4240241408 | bytes 19898368 | tf_op jit(solution)/shard_map/hiy,qy->hiq/dot_general | solution.py:159
  213.3 2.9 copy.101
  216.2 4.4 all-to-all-start.1
  220.6 20.1 %all-to-all-done.1 = bf16[7,128,768]{1,0,2:T(8,128)(2,1)} async-done(((bf16[7,128,768]{1,0,2:T(8,128)(2,1)}), bf16[7,128,768]{1,0,2:T(8,128)(2,1)}, u32[]{:S(2)}, u32[]{:S(2)}) %all-to-all-start.1) | async-done | bytes 1376288 | tf_op jit(solution)/shard_map/all_to_all | solution.py:175
  240.7 3.7 copy.103
  244.4 3.6 reshape.145
  251.8 70.3 %while.27 = (s32[]{:T(128)}, bf16[7,512,3,64]{1,3,2,0:T(8,128)(2,1)}, bf16[7,512,3,64]{1,3,2,0:T(8,128)(2,1)}, bf16[7,512,3,64]{1,3,2,0:T(8,128)(2,1)}, bf16[7,5...) while((s32[]{:T(128)}, ...), condition=%wide.region_14.15_spmd, body=%wide.region_12.14_spmd.sunk | while | flops 510884352 | bytes 25598580 | solution.py:178
  322.1 8.4 fusion.94
  330.5 2.9 copy.122
  333.6 9.4 %convolution_convert_fusion = bf16[7,512,768]{2,1,0:T(8,128)(2,1)} fusion(bf16[7,512,192]{1,2,0:T(8,128)(2,1)} %bitcast.34, bf16[7,512,192]{1,2,0:T(8,128)(2,1)} %bitcast.183, bf16[7,512,192]{1,2,0:T(8,128)(2,1)S(1)} %bitcast.179, bf16[768,192]{0,1:T(8,128)(2,1)S(1)} %copy-done.20, bf16[768,192]{0,1:T(8,128)(2,1)S(1)} %copy-done.21, ...), kind=kOutput, calls=%fused_computation.107 | convolution fusion | flops 3188686848 | bytes 10518528 | tf_op jit(solution)/shard_map/hiy,qy->hiq/dot_general | solution.py:191
  344.3 4.2 convolution_bitcast_fusion.3
  348.6 9.8 %convolution_bitcast_fusion = f32[3072,768]{1,0:T(8,128)} fusion(bf16[7,128,3072]{2,1,0:T(8,128)(2,1)} %copy-done.8, bf16[7,128,768]{2,1,0:T(8,128)(2,1)} %copy-done.11), kind=kOutput, calls=%fused_computation.90 | convolution fusion | flops 4227858432 | bytes 16318464 | tf_op jit(solution)/shard_map/zrp,zrx->px/dot_general | solution.py:147
  358.4 10.7 %convolution_bitcast_fusion.1 = f32[768,3072]{0,1:T(8,128)} fusion(bf16[7,128,3072]{2,1,0:T(8,128)(2,1)} %get-tuple-element.273, f32[7,128,768]{2,1,0:T(8,128)} %copy-done.2, f32[768]{0:T(1024)S(1)} %convert_element_type.124, f32[768]{0:T(1024)S(1)} %convert_element_type.123, f32[7,128]{1,0:T(8,128)S(1)} %add_rsqrt_fusion.1, ...), kind=kOutput, calls=%fused_computation.91 | convolution fusion | flops 4231299072 | bytes 17708032 | tf_op jit(solution)/shard_map/vrb,vrm->bm/dot_general | solution.py:155
  372.9 41.0 %all-reduce = (f32[768]{0:T(1024)}, f32[768]{0:T(1024)}, f32[768]{0:T(1024)}, f32[768]{0:T(1024)}, f32[768]{0:T(1024)}, /*index=5*/f32[3072]{0:T(1024)}, f32[768]{0:T(1024)}, f32[768]{0:T(1024)}, f32[768]{0:T(1024)}) all-reduce(f32[768]{0:T(1024)S(1)} %dynamic_update_slice.23, ...), channel_id=1, replica_groups=mesh['dp'=8,'head'=4] {'dp','head'}, use_global_device_ids=true, to_apply=%region_18.19 | all-reduce | flops 9216 | bytes 73728 | tf_op jit(solution)/shard_map/psum | solution.py:209
  415.8 40.1 %reduce-scatter.8.cloned.1.call-done = bf16[7,128,768]{2,1,0:T(8,128)(2,1)} async-done(((bf16[7,512,768]{2,1,0:T(8,128)(2,1)}), bf16[7,128,768]{2,1,0:T(8,128)(2,1)}) %reduce-scatter.8.cloned.1.call-update) | async-done | bytes 1376272 | tf_op jit(solution)/shard_map/reduce_scatter | solution.py:195
  455.9 4.6 convert_add_fusion
  460.5 100.2 %reduce-scatter.10.cloned.1.call-done = f32[768,24]{0,1:T(8,128)} async-done(((f32[768,768]{0,1:T(8,128)}), f32[768,24]{0,1:T(8,128)}) %reduce-scatter.10.cloned.1.call-update) | async-done | bytes 73744 | tf_op jit(solution)/shard_map/reduce_scatter | solution.py:224
  560.7 142.0 %reduce-scatter.14.cloned.1.call-done = f32[96,768]{1,0:T(8,128)} async-done(((f32[3072,768]{1,0:T(8,128)}), f32[96,768]{1,0:T(8,128)}) %reduce-scatter.14.cloned.1.call-update) | async-done | bytes 294928 | tf_op jit(solution)/shard_map/reduce_scatter | solution.py:226
  702.7 141.0 %reduce-scatter.12.cloned.1.call-done = f32[768,96]{0,1:T(8,128)} async-done(((f32[768,3072]{0,1:T(8,128)}), f32[768,96]{0,1:T(8,128)}) %reduce-scatter.12.cloned.1.call-update) | async-done | bytes 294928 | tf_op jit(solution)/shard_map/reduce_scatter | solution.py:225
  (194 shorter events, 131.2 us)
Async XLA Ops:
  7.2 132.3 %copy-start = (bf16[768,768]{1,0:T(8,128)(2,1)S(1)}, bf16[768,768]{1,0:T(8,128)(2,1)}, u32[]{:S(2)}) copy-start(bf16[768,768]{1,0:T(8,128)(2,1)} %param.29) | copy-start | bytes 3538948
  7.2 47.0 %all-gather.2.cloned.1.call-start = ((), (), s32[]{:S(2)}) async-start(), calls=%async_computation.7 | async-start | bytes 6881280 | tf_op jit(solution)/shard_map/all_gather | solution.py:98
  103.3 5.2 copy-start.14
  103.3 5.2 copy-start.15
  103.3 5.2 copy-start.13
  103.3 5.2 copy-start.16
  103.4 5.2 copy-start.17
  103.4 5.2 copy-start.18
  103.4 5.2 copy-start.19
  103.4 30.8 %all-to-all-start = ((bf16[7,512,192]{2,0,1:T(8,128)(2,1)}), bf16[7,512,192]{2,0,1:T(8,128)(2,1)}, u32[]{:S(2)}, u32[]{:S(2)}) async-start(bf16[7,512,192]{2,0,1:T(8,128)(2,1)} %copy.97), calls=%async_computation | async-start | bytes 4194304 | tf_op jit(solution)/shard_map/all_to_all | solution.py:119
  137.7 1.8 copy-start.4
  139.5 1.5 copy-start.5
  141.0 67.2 %copy-start.2 = (f32[7,128,768]{2,1,0:T(8,128)}, f32[7,128,768]{2,1,0:T(8,128)S(1)}, u32[]{:S(2)}) copy-start(f32[7,128,768]{2,1,0:T(8,128)S(1)} %get-tuple-element.267) | copy-start | bytes 8257540
  141.1 37.1 %slice-start = ((s8[4718592]{0:T(1024)(128)(4,1)}), s8[4194304]{0:T(1024)(128)(4,1)S(1)}, s32[]{:S(2)}) async-start(s8[4718592]{0:T(1024)(128)(4,1)} %bitcast.184), calls=%async_computation.13 | async-start | bytes 8388608
  141.5 36.7 %slice-start.1 = ((s8[4718592]{0:T(1024)(128)(4,1)}), s8[524288]{0:T(1024)(128)(4,1)S(1)}, s32[]{:S(2)}) async-start(s8[4718592]{0:T(1024)(128)(4,1)} %bitcast.184), calls=%async_computation.14 | async-start | bytes 1048576
  178.2 4.8 copy-start.8
  183.1 1.3 copy-start.7
  187.9 10.8 %copy-start.11 = (bf16[7,128,768]{2,1,0:T(8,128)(2,1)}, bf16[7,128,768]{2,1,0:T(8,128)(2,1)S(1)}, u32[]{:S(2)}) copy-start(bf16[7,128,768]{2,1,0:T(8,128)(2,1)S(1)} %get-tuple-element.253) | copy-start | bytes 4128772
  208.2 1.5 copy-start.3
  216.2 24.5 %all-to-all-start.1 = ((bf16[7,128,768]{1,0,2:T(8,128)(2,1)}), bf16[7,128,768]{1,0,2:T(8,128)(2,1)}, u32[]{:S(2)}, u32[]{:S(2)}) async-start(bf16[7,128,768]{1,0,2:T(8,128)(2,1)} %copy.101), calls=%async_computation.1 | async-start | bytes 3145728 | tf_op jit(solution)/shard_map/all_to_all | solution.py:175
  220.6 193.3 %reduce-scatter.16.cloned.1.call-start = ((), (), s32[]{:S(2)}) async-start(), calls=%async_computation.12 | async-start | bytes 2211840
  330.5 3.0 copy-start.9
  330.5 3.0 copy-start.20
  330.5 3.0 copy-start.21
  330.5 3.1 copy-start.22
  333.5 122.5 %reduce-scatter.8.cloned.1.call-start = ((), (), s32[]{:S(2)}) async-start(), calls=%async_computation.8 | async-start | bytes 6881280 | tf_op jit(solution)/shard_map/reduce_scatter | solution.py:195
  343.0 1.3 copy-start.6
  343.0 217.7 %reduce-scatter.10.cloned.1.call-start = ((), (), s32[]{:S(2)}) async-start(), calls=%async_computation.9 | async-start | bytes 2433024 | tf_op jit(solution)/shard_map/reduce_scatter | solution.py:224
  348.5 354.2 %reduce-scatter.14.cloned.1.call-start = ((), (), s32[]{:S(2)}) async-start(), calls=%async_computation.11 | async-start | bytes 9732096 | tf_op jit(solution)/shard_map/reduce_scatter | solution.py:226
  358.3 485.4 %reduce-scatter.12.cloned.1.call-start = ((), (), s32[]{:S(2)}) async-start(), calls=%async_computation.10 | async-start | bytes 9732096 | tf_op jit(solution)/shard_map/reduce_scatter | solution.py:225
  369.1 1.3 copy-start.10
  413.9 429.8 %copy-start.1 = (bf16[768,768]{1,0:T(8,128)(2,1)S(1)}, bf16[768,768]{1,0:T(8,128)(2,1)}, u32[]{:S(2)}) copy-start(bf16[768,768]{1,0:T(8,128)(2,1)} %param.29) | copy-start | bytes 3538948
  (1 other events, 1.1 us)
Sparse Core Ops, SparseCore 0:
  9.6 44.6 all-gather.1
  333.6 66.9 reduce-scatter.15
  403.3 52.6 reduce-scatter.7
  461.7 99.0 reduce-scatter.9
  568.1 134.6 reduce-scatter.13
  709.1 134.6 reduce-scatter.11
where the time goes:
time: 857 us; the launch traced here: 851 us
  waiting for transfers between devices  514 us (60%)
  matrix products  182 us (21%)
  other arithmetic  53.1 us (6%)
  blocking collectives  41 us (5%)
  local copies, waits for them, and re-layouts  35.8 us (4%)
  between operations  15 us (2%)
  starting transfers between devices  9.71 us (1%)
    reduce_scatter x1, waiting for transfers between devices, on_device(): lax.psum_scatter(outer_weight_grad, ('dp', 'head'), scatter_dimension=0,...  142 us
    reduce_scatter x1, waiting for transfers between devices, on_device(): lax.psum_scatter(inner_weight_grad, ('dp', 'head'), scatter_dimension=1,...  141 us
    reduce_scatter x1, waiting for transfers between devices, on_device(): lax.psum_scatter(output_weight_grad, ('dp', 'head'), scatter_dimension=1,...  100 us
    all_gather x1, waiting for transfers between devices, on_device(): gathered_rows = lax.all_gather(inputs, 'head', axis=1, tiled=True)  44.3 us
    psum x1, blocking collectives, on_device(): lax.psum((query_bias_full, value_bias_full, output_bias_grad, first_gain_...  41 us
    reduce_scatter x1, waiting for transfers between devices, on_device(): lax.psum_scatter(partial_gradient.astype(jnp.bfloat16), 'head', scatter_d...  40.1 us
    dot_general x14, matrix products, masked_scores(): jnp.einsum('qhd,khd->hqk', queries, key_rows, preferred_element_type=jnp....  26.1 us
    all_to_all x1, waiting for transfers between devices, on_device(): lax.all_to_all(context, 'head', split_axis=1, concat_axis=2, tiled=True)  25.6 us
  transfers between devices with their start and end apart: 8, of which 7 were waited for; matrix products, arithmetic and copies ran while one was open for 5% of the time, Pallas kernels for 0%

commit v1 on v0

--- a/solution.py
+++ b/solution.py
@@ -1,6 +1,11 @@
+import functools
+
 import jax
 import jax.numpy as jnp
+import numpy as np
 from jax import lax
+from jax.experimental import pallas as pl
+from jax.experimental.pallas import tpu as pltpu
 from jax.sharding import PartitionSpec as P
 
 HEAD_DIM = 64
@@ -9,6 +14,226 @@
 EPSILON = 1e-12
 MASKED = -1e30
 SCALE = 0.125
+
+
+def mesh_steps(sizes, axis):
+    return [(axis, 1 << k) for k in range(sizes[axis].bit_length() - 1)]
+
+
+def all_steps(sizes):
+    head = mesh_steps(sizes, "head")
+    return head[:1] + mesh_steps(sizes, "dp") + head[1:]
+
+
+def bit_of(step):
+    return lax.rem(lax.axis_index(step[0]) // step[1], 2)
+
+
+def partner_of(step):
+    return {step[0]: lax.axis_index(step[0]) + step[1] * (1 - 2 * bit_of(step))}
+
+
+def chunk_order(sizes, steps):
+    both = any(axis == "head" for axis, _ in steps)
+    order = []
+    for place in range(1 << len(steps)):
+        at = {"dp": 0, "head": 0}
+        for level, (axis, width) in enumerate(steps):
+            if (place >> (len(steps) - 1 - level)) & 1:
+                at[axis] += width
+        order.append(at["dp"] * sizes["head"] + at["head"] if both else at["dp"])
+    return order
+
+
+def halves(step, count):
+    bit = bit_of(step)
+    return bit * (count // 2), (1 - bit) * (count // 2)
+
+
+class Scatter:
+    def __init__(self, steps, source, landing, send, recv, result):
+        self.steps, self.source, self.landing = steps, source, landing
+        self.send_sem, self.recv_sem, self.result = send, recv, result
+        self.parts = source.shape[0]
+
+    def held(self, level):
+        return self.source if level == 0 else self.landing[level - 1]
+
+    def copy(self, part, level):
+        block = self.held(level)
+        count = block.shape[1]
+        _, other = halves(self.steps[level], count)
+        return pltpu.make_async_remote_copy(
+            src_ref=block.at[part, pl.ds(other, count // 2)],
+            dst_ref=self.landing[level].at[part],
+            send_sem=self.send_sem.at[part, level],
+            recv_sem=self.recv_sem.at[part, level],
+            device_id=partner_of(self.steps[level]),
+            device_id_type=pl.DeviceIdType.MESH,
+        )
+
+    def start(self, part, level):
+        self.copy(part, level).start()
+
+    def land(self, part, level):
+        self.copy(part, level).wait_recv()
+        block, landed = self.held(level), self.landing[level]
+        count = block.shape[1]
+        mine, _ = halves(self.steps[level], count)
+        last = level == len(self.steps) - 1
+
+        def add(i, carry):
+            total = landed[part, i].astype(jnp.float32) + block[part, mine + i].astype(jnp.float32)
+            if last:
+                self.result[part] = total
+            else:
+                landed[part, i] = total.astype(landed.dtype)
+            return carry
+
+        lax.fori_loop(0, count // 2, add, 0)
+
+    def finish(self):
+        for part in range(self.parts):
+            for level in range(len(self.steps)):
+                self.copy(part, level).wait_send()
+
+
+class Everywhere:
+    def __init__(self, steps, source, landing, total, send, recv, result):
+        self.steps, self.source, self.landing, self.total = steps, source, landing, total
+        self.send_sem, self.recv_sem, self.result = send, recv, result
+
+    def held(self, level):
+        return self.source if level == 0 else self.total.at[level - 1]
+
+    def copy(self, level):
+        return pltpu.make_async_remote_copy(
+            src_ref=self.held(level),
+            dst_ref=self.landing.at[level],
+            send_sem=self.send_sem.at[level],
+            recv_sem=self.recv_sem.at[level],
+            device_id=partner_of(self.steps[level]),
+            device_id_type=pl.DeviceIdType.MESH,
+        )
+
+    def land(self, level):
+        self.copy(level).wait_recv()
+        total = self.held(level)[...] + self.landing[level]
+        if level == len(self.steps) - 1:
+            self.result[...] = total
+        else:
+            self.total[level] = total
+
+    def finish(self):
+        for level in range(len(self.steps)):
+            self.copy(level).wait_send()
+
+
+def greet(steps):
+    barrier = pltpu.get_barrier_semaphore()
+    for step in steps:
+        pl.semaphore_signal(
+            barrier, inc=1, device_id=partner_of(step), device_id_type=pl.DeviceIdType.MESH
+        )
+    pl.semaphore_wait(barrier, len(steps))
+
+
+def reduce_kernel(steps, dp_steps, wide_ref, head_ref, small_ref, wide_out, head_out, small_out, *scratch):
+    count = len(steps)
+    wide_land, scratch = scratch[:count], scratch[count:]
+    head_land, scratch = scratch[: len(dp_steps)], scratch[len(dp_steps) :]
+    small_land, small_total, sems = scratch[0], scratch[1], scratch[2:]
+    wide = Scatter(steps, wide_ref, wide_land, sems[0], sems[1], wide_out)
+    head = Scatter(dp_steps, head_ref, head_land, sems[2], sems[3], head_out)
+    small = Everywhere(steps, small_ref, small_land, small_total, sems[4], sems[5], small_out)
+    greet(steps)
+    for part in range(wide.parts):
+        wide.start(part, 0)
+    small.copy(0).start()
+    for part in range(head.parts):
+        head.start(part, 0)
+    for turn in range(wide.parts + count - 1):
+        for level in reversed(range(count)):
+            part = turn - level
+            if 0 <= part < wide.parts:
+                wide.land(part, level)
+                if level + 1 < count:
+                    wide.start(part, level + 1)
+        for level in reversed(range(len(dp_steps))):
+            part = turn - level
+            if 0 <= part < head.parts:
+                head.land(part, level)
+                if level + 1 < len(dp_steps):
+                    head.start(part, level + 1)
+        if turn < count:
+            small.land(turn)
+            if turn + 1 < count:
+                small.copy(turn + 1).start()
+    for turn in range(wide.parts + count - 1, count):
+        small.land(turn)
+        if turn + 1 < count:
+            small.copy(turn + 1).start()
+    wide.finish()
+    head.finish()
+    small.finish()
+
+
+def reduce_all(sizes, wide, head, small):
+    steps, dp_steps = all_steps(sizes), mesh_steps(sizes, "dp")
+    count = len(steps)
+
+    def landing(array, length):
+        parts, n = array.shape[:2]
+        return [
+            pltpu.VMEM((parts, n >> (level + 1)) + array.shape[2:], array.dtype)
+            for level in range(length)
+        ]
+
+    dma = pltpu.SemaphoreType.DMA
+    vmem = pl.BlockSpec(memory_space=pltpu.VMEM)
+    return pl.pallas_call(
+        functools.partial(reduce_kernel, steps, dp_steps),
+        out_shape=[
+            jax.ShapeDtypeStruct((wide.shape[0],) + wide.shape[2:], jnp.float32),
+            jax.ShapeDtypeStruct((head.shape[0],) + head.shape[2:], jnp.float32),
+            jax.ShapeDtypeStruct(small.shape, jnp.float32),
+        ],
+        in_specs=[vmem] * 3,
+        out_specs=[vmem] * 3,
+        scratch_shapes=landing(wide, count)
+        + landing(head, len(dp_steps))
+        + [
+            pltpu.VMEM((count,) + small.shape, jnp.float32),
+            pltpu.VMEM((count,) + small.shape, jnp.float32),
+            dma((wide.shape[0], count)),
+            dma((wide.shape[0], count)),
+            dma((head.shape[0], len(dp_steps))),
+            dma((head.shape[0], len(dp_steps))),
+            dma((count,)),
+            dma((count,)),
+        ],
+        compiler_params=pltpu.CompilerParams(
+            collective_id=0, has_side_effects=True, vmem_limit_bytes=48 * 1024 * 1024
+        ),
+    )(wide, head, small)
+
+
+def round_up(value, unit):
+    return -(-value // unit) * unit
+
+
+def part_rows(rows):
+    return 32 if rows % 32 == 0 else 16
+
+
+def pack_chunks(sizes, steps, arrays):
+    n = 1 << len(steps)
+    joined = jnp.concatenate([a.reshape(n, a.shape[0] // n, a.shape[1]) for a in arrays], axis=1)
+    rows = round_up(joined.shape[1], 32 if joined.shape[1] > 16 else 16)
+    joined = jnp.pad(joined, ((0, 0), (0, rows - joined.shape[1]), (0, 0)))
+    unit = part_rows(rows)
+    joined = joined[np.array(chunk_order(sizes, steps))]
+    return joined.reshape(n, rows // unit, unit, joined.shape[2]).transpose(1, 0, 2, 3)
 
 
 def normalize(hidden, gain, shift):
@@ -72,6 +297,7 @@
 
 
 def on_device(
+    sizes,
     inputs,
     lengths,
     query_weight,
@@ -146,15 +372,15 @@
     outer_bias_grad = jnp.sum(branch_gradient.astype(jnp.float32), axis=(0, 1))
     outer_weight_grad = jnp.einsum(
         "zrp,zrx->px", active_lower_part, branch_gradient, preferred_element_type=jnp.float32
-    )
+    ).astype(jnp.bfloat16)
     active_gradient = jnp.einsum(
         "ofv,jv->ofj", branch_gradient, contract_weight, preferred_element_type=jnp.float32
     )
     hidden_gradient = (active_gradient * gelu_slope(hidden_in)).astype(jnp.bfloat16)
     inner_bias_grad = jnp.sum(hidden_gradient.astype(jnp.float32), axis=(0, 1))
     inner_weight_grad = jnp.einsum(
-        "vrb,vrm->bm", first_lower_part, hidden_gradient, preferred_element_type=jnp.float32
-    )
+        "vrb,vrm->mb", first_lower_part, hidden_gradient, preferred_element_type=jnp.float32
+    ).astype(jnp.bfloat16)
     dfirst = (
         jnp.einsum(
             "hiy,qy->hiq", hidden_gradient, expand_weight, preferred_element_type=jnp.float32
@@ -167,8 +393,8 @@
     attended_gradient = dsum.astype(jnp.bfloat16)
     output_bias_grad = jnp.sum(attended_gradient.astype(jnp.float32), axis=(0, 1))
     output_weight_grad = jnp.einsum(
-        "zrp,zrx->px", context_token_rows, attended_gradient, preferred_element_type=jnp.float32
-    )
+        "zrp,zrx->xp", context_token_rows, attended_gradient, preferred_element_type=jnp.float32
+    ).astype(jnp.bfloat16)
     dcontext = jnp.einsum(
         "ofv,jv->ofj", attended_gradient, attention_out_weight, preferred_element_type=jnp.float32
     ).astype(jnp.bfloat16)
@@ -205,26 +431,35 @@
     value_bias_full = lax.dynamic_update_slice_in_dim(
         zeros_width, value_bias_grad, head_index * local_width, 0
     )
-    head_part = lax.psum_scatter(combined_gradient, "dp", scatter_dimension=0, tiled=True)
-    small_sums = lax.psum(
-        (
-            query_bias_full,
-            value_bias_full,
-            output_bias_grad,
-            first_gain_grad,
-            first_shift_grad,
-            inner_bias_grad,
-            outer_bias_grad,
-            second_gain_grad,
-            second_shift_grad,
-        ),
-        ("dp", "head"),
-    )
-    shared = (
-        lax.psum_scatter(output_weight_grad, ("dp", "head"), scatter_dimension=1, tiled=True),
-        lax.psum_scatter(inner_weight_grad, ("dp", "head"), scatter_dimension=1, tiled=True),
-        lax.psum_scatter(outer_weight_grad, ("dp", "head"), scatter_dimension=0, tiled=True),
-    )
+    steps, dp_steps = all_steps(sizes), mesh_steps(sizes, "dp")
+    sums = [
+        query_bias_full,
+        value_bias_full,
+        output_bias_grad,
+        first_gain_grad,
+        first_shift_grad,
+        inner_bias_grad,
+        outer_bias_grad,
+        second_gain_grad,
+        second_shift_grad,
+    ]
+    small = jnp.concatenate(sums)
+    small = jnp.pad(small, (0, round_up(small.shape[0], 8 * model_width) - small.shape[0]))
+    wide, head_part, small = reduce_all(
+        sizes,
+        pack_chunks(sizes, steps, [outer_weight_grad, inner_weight_grad, output_weight_grad]),
+        pack_chunks(sizes, dp_steps, [combined_gradient.astype(jnp.bfloat16)]),
+        small.reshape(-1, model_width),
+    )
+    wide = wide.reshape(-1, model_width)
+    n = 1 << len(steps)
+    inner_rows, output_rows = expand_weight.shape[1] // n, model_width // n
+    head_part = head_part.reshape(-1, 3 * local_width)[: model_width // (1 << len(dp_steps))]
+    small = small.reshape(-1)
+    small_sums, at = [], 0
+    for piece in sums:
+        small_sums.append(small[at : at + piece.shape[0]])
+        at += piece.shape[0]
     return (
         output,
         input_gradient,
@@ -233,13 +468,13 @@
         head_part[:, local_width : 2 * local_width],
         head_part[:, 2 * local_width :],
         small_sums[1],
-        shared[0],
+        wide[2 * inner_rows : 2 * inner_rows + output_rows].T,
         small_sums[2],
         small_sums[3],
         small_sums[4],
-        shared[1],
+        wide[inner_rows : 2 * inner_rows].T,
         small_sums[5],
-        shared[2],
+        wide[:inner_rows],
         small_sums[6],
         small_sums[7],
         small_sums[8],
@@ -287,5 +522,5 @@
         P(),
     )
     return jax.shard_map(
-        on_device, mesh=mesh, in_specs=in_specs, out_specs=out_specs, check_vma=False
-    )
+        functools.partial(on_device, dict(mesh.shape)), mesh=mesh, in_specs=in_specs, out_specs=out_specs, check_vma=False
+    )

time: 857 us -> 505 us (0.59)
  waiting for transfers between devices: 514 us -> 90.6 us
  Pallas kernels: 0 us -> 95.2 us
  blocking collectives: 41 us -> 0 us
  local copies, waits for them, and re-layouts: 35.8 us -> 55.8 us
    reduce_scatter x3 -> x0, waiting for transfers between devices: 383 us -> none  [the longest x1 142 us: on_device(): lax.psum_scatter(outer_weight_grad, ('dp', 'head'), scatter_dimension=0,...]
    pallas_call x0 -> x1, Pallas kernels: none -> 95.2 us  [reduce_all(): pl.pallas_call(functools.partial(reduce_kernel, steps, dp_steps), out_sha...]
    psum x1 -> x0, blocking collectives: 41 us -> none  [on_device(): lax.psum((query_bias_full, value_bias_full, output_bias_grad, first_gain_...]
    reduce_scatter x1, waiting for transfers between devices: 40.1 us -> 0.01 us  [on_device(): lax.psum_scatter(partial_gradient.astype(jnp.bfloat16), 'head', scatter_d...]
    gather x0 -> x3, local copies, waits for them, and re-layouts: none -> 16.6 us  [pack_chunks(): joined = joined[np.array(chunk_order(sizes, steps))]]
  transfers between devices with their start and end apart: 8 -> 4, of which waited for: 7 -> 3; matrix products, arithmetic and copies ran while one was open for 5% -> 12% of each run, Pallas kernels for 0% -> 19%
where the time goes in v1:
time: 505 us; the launch traced here: 499 us
  matrix products  175 us (35%)
  Pallas kernels  95.2 us (19%)
  waiting for transfers between devices  90.6 us (18%)
  other arithmetic  58.1 us (12%)
  local copies, waits for them, and re-layouts  55.8 us (11%)
  between operations  15.2 us (3%)
  starting transfers between devices  9.48 us (2%)
    pallas_call x1, Pallas kernels, reduce_all(): pl.pallas_call(functools.partial(reduce_kernel, steps, dp_steps), out_sha...  95.2 us
    all_gather x1, waiting for transfers between devices, on_device(): gathered_rows = lax.all_gather(inputs, 'head', axis=1, tiled=True)  44.3 us
    dot_general x14, matrix products, masked_scores(): jnp.einsum('qhd,khd->hqk', queries, key_rows, preferred_element_type=jnp....  26.1 us
    all_to_all x1, waiting for transfers between devices, on_device(): lax.all_to_all(context, 'head', split_axis=1, concat_axis=2, tiled=True)  25.6 us
    convert_element_type x1, other arithmetic, on_device(): jax.nn.gelu(hidden_in, approximate=False).astype(jnp.bfloat16)  25.6 us
    all_to_all x1, waiting for transfers between devices, on_device(): lax.all_to_all(dcontext, 'head', split_axis=2, concat_axis=1, tiled=True)  20.1 us
    dot_general x7, matrix products, attend(): jnp.einsum('hqk,khd->qhd', weights, values, preferred_element_type=jnp.fl...  18 us
    gather x3, local copies, waits for them, and re-layouts, pack_chunks(): joined = joined[np.array(chunk_order(sizes, steps))]  16.6 us
  transfers between devices with their start and end apart: 4, of which 3 were waited for; matrix products, arithmetic and copies ran while one was open for 12% of the time, Pallas kernels for 19%

profile of v1, /device:TPU:0, one launch (start us, length us, event | category | flops | bytes accessed | tf_op | source)
XLA Modules:
  0.0 499.5 jit_solution(12645637767265847889)
XLA Ops:
  10.0 44.3 %all-gather.2.cloned.1.call-done = bf16[7,512,768]{2,1,0:T(8,128)(2,1)} async-done(((bf16[7,128,768]{2,1,0:T(8,128)(2,1)}), bf16[7,512,768]{2,1,0:T(8,128)(2,1)}) %all-gather.2.cloned.1.call-update) | async-done | bytes 5505040 | tf_op jit(solution)/shard_map/all_gather | solution.py:324
  54.3 5.8 %convolution_bitcast_fusion = f32[7,512,576]{1,2,0:T(8,128)S(1)} fusion(bf16[7,512,768]{2,1,0:T(8,128)(2,1)} %all-gather.2.cloned.1.call-done, bf16[768,192]{0,1:T(8,128)(2,1)} %param.31, bf16[768,192]{0,1:T(8,128)(2,1)} %param.30, bf16[768,192]{0,1:T(8,128)(2,1)} %param.28), kind=kOutput, calls=%fused_computation.110 | convolution fusion | flops 3173548032 | bytes 14647296 | tf_op jit(solution)/shard_map/bhj,ja->bha/dot_general | solution.py:327
  63.9 35.1 %while.26 = (s32[]{:T(128)}, bf16[7,512,3,64]{1,3,2,0:T(8,128)(2,1)}, f32[7,3,512,1]{2,1,3,0:T(4,128)S(1)}, bf16[7,512,3,64]{1,3,2,0:T(8,128)(2,1)}, pred[7,512]...) while((s32[]{:T(128)}, ...), condition=%wide.region_3.4_spmd, body=%wide.region_0.3_spmd.sunk | while | flops 210860544 | bytes 10283613 | solution.py:343
  66.4 2.6 fusion.143
  71.4 2.6 fusion.143
  76.4 2.6 fusion.143
  99.0 4.3 copy.98
  103.4 5.1 %all-to-all-start = ((bf16[7,512,192]{2,0,1:T(8,128)(2,1)}), bf16[7,512,192]{2,0,1:T(8,128)(2,1)}, u32[]{:S(2)}, u32[]{:S(2)}) async-start(bf16[7,512,192]{2,0,1:T(8,128)(2,1)} %copy.98), calls=%async_computation | async-start | bytes 4194304 | tf_op jit(solution)/shard_map/all_to_all | solution.py:345
  108.6 25.6 %all-to-all-done = bf16[7,512,192]{2,0,1:T(8,128)(2,1)} async-done(((bf16[7,512,192]{2,0,1:T(8,128)(2,1)}), bf16[7,512,192]{2,0,1:T(8,128)(2,1)}, u32[]{:S(2)}, u32[]{:S(2)}) %all-to-all-start) | async-done | bytes 1376288 | tf_op jit(solution)/shard_map/all_to_all | solution.py:345
  134.2 3.5 copy.121
  141.5 11.1 %fusion.86 = (u8[128,3072]{1,0:T(8,128)(4,1)S(1)}, u8[128,3072]{1,0:T(8,128)(4,1)S(1)}, f32[7,128,3072]{2,1,0:T(8,128)S(1)}) fusion(f32[3072]{0:T(1024)S(1)} %convert_element_type.145, bf16[768,3072]{1,0:T(8,128)(2,1)} %param.37, f32[7,128,768]{2,1,0:T(8,128)S(1)} %get-tuple-element.189, f32[768]{0:T(1024)S(1)} %convert_element_type.143, ...), kind=kOutput, calls=%fused_computation.136 | convolution fusion | flops 4269047808 | bytes 19293184 | tf_op jit(solution)/shard_map/bhj,ja->bha/dot_general | solution.py:356
  152.6 25.6 %fusion.56 = bf16[7,128,3072]{2,1,0:T(8,128)(2,1)S(1)} fusion(f32[7,128,3072]{2,1,0:T(8,128)S(1)} %get-tuple-element.190, f32[3072]{0:T(1024)S(1)} %convert_element_type.145, u8[128,3072]{1,0:T(8,128)(4,1)S(1)} %get-tuple-element.121, u8[128,3072]{1,0:T(8,128)(4,1)S(1)} %get-tuple-element.120), kind=kLoop, calls=%fused_computation.66 | loop fusion | flops 195428352 | bytes 17313792 | tf_op jit(solution)/shard_map/convert_element_type | solution.py:359
  178.2 4.8 fusion.109
  187.9 11.0 %convert_reduce_fusion = (f32[3072]{0:T(1024)S(1)}, bf16[7,128,3072]{2,1,0:T(8,128)(2,1)}) fusion(f32[7,128,3072]{2,1,0:T(8,128)S(1)} %get-tuple-element.190, f32[3072]{0:T(1024)S(1)} %convert_element_type.145, bf16[7,128,768]{2,1,0:T(8,128)(2,1)S(1)} %get-tuple-element.173, bf16[3072,768]{1,0:T(8,128)(2,1)S(1)} %bitcast.218), kind=kOutput, calls=%fused_computation.79 | convolution fusion | flops 4263638016 | bytes 22634496 | tf_op jit(solution)/shard_map/ofv,jv->ofj/dot_general | solution.py:376
  198.9 9.5 %multiply_reduce_fusion.1 = (f32[768]{0:T(1024)S(1)}, f32[7,128]{1,0:T(8,128)S(1)}, f32[7,128]{1,0:T(8,128)S(1)}, f32[768]{0:T(1024)S(1)}, f32[7,128,768]{2,1,0:T(8,128)S(1)}) fusion(f32[7,128,768]{2,1,0:T(8,128)S(1)} %get-tuple-element.189, f32[7,128]{1,0:T(8,128)S(1)} %add_rsqrt_fusion.1, f32[7,128]{1,0:T(8,128)S(1)} %broadcast_multiply_fusion.5, ...), kind=kOutput, calls=%fused_computation.122 | convolution fusion | flops 4240241408 | bytes 19898368 | tf_op jit(solution)/shard_map/hiy,qy->hiq/dot_general | solution.py:385
  213.4 2.9 copy.102
  216.2 4.3 all-to-all-start.1
  220.6 20.1 %all-to-all-done.1 = bf16[7,128,768]{1,0,2:T(8,128)(2,1)} async-done(((bf16[7,128,768]{1,0,2:T(8,128)(2,1)}), bf16[7,128,768]{1,0,2:T(8,128)(2,1)}, u32[]{:S(2)}, u32[]{:S(2)}) %all-to-all-start.1) | async-done | bytes 1376288 | tf_op jit(solution)/shard_map/all_to_all | solution.py:401
  240.7 3.7 copy.104
  244.4 3.6 reshape.184
  251.7 70.4 %while.27 = (s32[]{:T(128)}, bf16[7,512,3,64]{1,3,2,0:T(8,128)(2,1)}, bf16[7,512,3,64]{1,3,2,0:T(8,128)(2,1)}, bf16[7,512,3,64]{1,3,2,0:T(8,128)(2,1)}, bf16[7,5...) while((s32[]{:T(128)}, ...), condition=%wide.region_14.15_spmd, body=%wide.region_12.14_spmd.sunk | while | flops 510884352 | bytes 25598580 | solution.py:404
  322.2 9.5 %convolution_convert_fusion = bf16[7,512,768]{2,1,0:T(8,128)(2,1)} fusion(bf16[7,512,192]{1,2,0:T(8,128)(2,1)} %bitcast.34, bf16[7,512,192]{1,2,0:T(8,128)(2,1)} %bitcast.212, bf16[7,512,192]{1,2,0:T(8,128)(2,1)} %bitcast.204, bf16[768,192]{0,1:T(8,128)(2,1)S(1)} %copy-done.23, bf16[768,192]{0,1:T(8,128)(2,1)S(1)} %copy-done.24, ...), kind=kOutput, calls=%fused_computation.111 | convolution fusion | flops 3188686848 | bytes 10518528 | tf_op jit(solution)/shard_map/hiy,qy->hiq/dot_general | solution.py:417
  333.1 2.9 bitcast_convert_fusion.2
  336.0 9.2 %bitcast_convert_fusion.1 = bf16[3072,768]{1,0:T(8,128)(2,1)S(1)} fusion(bf16[7,128,3072]{2,1,0:T(8,128)(2,1)} %copy-done.9, bf16[7,128,768]{2,1,0:T(8,128)(2,1)S(1)} %copy-done.12), kind=kOutput, calls=%fused_computation.95 | convolution fusion | flops 4230217728 | bytes 11599872 | tf_op jit(solution)/shard_map/zrp,zrx->px/dot_general | solution.py:373
  345.3 6.5 %bitcast_convert_fusion = bf16[3072,768]{1,0:T(8,128)(2,1)S(1)} fusion(bf16[7,128,3072]{2,1,0:T(8,128)(2,1)S(1)} %bitcast.220, f32[7,128,768]{2,1,0:T(8,128)S(1)} %copy-done.3, f32[768]{0:T(1024)S(1)} %convert_element_type.143, f32[768]{0:T(1024)S(1)} %convert_element_type.142, f32[7,128]{1,0:T(8,128)S(1)} %add_rsqrt_fusion.1, ...), kind=kOutput, calls=%fused_computation.94 | convolution fusion | flops 4233658368 | bytes 12989440 | tf_op jit(solution)/shard_map/vrb,vrm->mb/dot_general | solution.py:381
  351.9 5.0 pad_maximum_fusion
  356.8 9.9 %gather_fusion = bf16[32,216,768]{2,1,0:T(8,128)(2,1)} fusion(bf16[32,216,768]{2,1,0:T(8,128)(2,1)} %pad_maximum_fusion, s32[1024]{0:T(1024)S(1)} %pad_clamp_fusion.1), kind=kCustom, calls=%fused_computation | custom fusion | bytes 21233792 | tf_op jit(solution)/shard_map/gather | solution.py:235
  366.7 5.9 %gather.10 = bf16[32,224,768]{2,1,0:T(8,128)(2,1)S(1)} pad(bf16[32,216,768]{2,1,0:T(8,128)(2,1)} %gather_fusion, bf16[]{:T(256)} %constant.71.clone.1), padding=0_0x0_8x0_0 | pad | bytes 21626882 | tf_op jit(solution)/shard_map/gather | solution.py:235
  372.7 5.3 %copy.125 = bf16[32,7,32,768]{3,2,0,1:T(8,128)(2,1)} copy(bf16[32,7,32,768]{3,2,1,0:T(8,128)(2,1)S(1)} %bitcast.199) | data formatting | bytes 22020096 | tf_op jit(solution)/shard_map/reshape | solution.py:236
  380.6 6.8 %fusion.94 = bf16[768,576]{0,1:T(8,128)(2,1)S(1)} fusion(bf16[7,512,768]{2,1,0:T(8,128)(2,1)} %all-gather.2.cloned.1.call-done, bf16[7,512,192]{1,2,0:T(8,128)(2,1)} %bitcast.34, bf16[7,512,192]{1,2,0:T(8,128)(2,1)} %bitcast.213, bf16[7,512,192]{1,2,0:T(8,128)(2,1)S(1)} %bitcast.205), kind=kOutput, calls=%fused_computation.146 | convolution fusion | flops 3183722496 | bytes 10518528 | tf_op jit(solution)/shard_map/vrb,vrm->bm/dot_general | solution.py:414
  388.9 95.2 %shard_map.341 = (f32[7,32,768]{2,1,0:T(8,128)S(1)}, f32[3,32,576]{2,1,0:T(8,128)S(1)}, f32[16,768]{1,0:T(8,128)S(1)}) custom-call(bf16[7,32,32,768]{3,2,1,0:T(8,128)(2,1)} %bitcast.198, bf16[3,8,32,576]{3,2,1,0:T(8,128)(2,1)S(1)} %bitcast.195, f32[16,768]{1,0:T(8,128)S(1)} %reshape.194.small_ref), custom_call_target="tpu_custom_call" | custom-call | tf_op jit(solution)/shard_map/pallas_call | solution.py:194
  487.6 4.6 convert_add_fusion
  (218 shorter events, 130.4 us)
Async XLA Ops:
  7.2 132.3 %copy-start = (bf16[768,768]{1,0:T(8,128)(2,1)S(1)}, bf16[768,768]{1,0:T(8,128)(2,1)}, u32[]{:S(2)}) copy-start(bf16[768,768]{1,0:T(8,128)(2,1)} %param.33) | copy-start | bytes 3538948
  7.2 47.0 %all-gather.2.cloned.1.call-start = ((), (), s32[]{:S(2)}) async-start(), calls=%async_computation.3 | async-start | bytes 6881280 | tf_op jit(solution)/shard_map/all_gather | solution.py:324
  103.4 5.1 %copy-start.15 = (bf16[768]{0:T(1024)(128)(2,1)S(1)}, bf16[768]{0:T(1024)(128)(2,1)}, u32[]{:S(2)}) copy-start(bf16[768]{0:T(1024)(128)(2,1)} %param.34) | copy-start | bytes 4612
  103.4 5.1 %copy-start.16 = (bf16[768]{0:T(1024)(128)(2,1)S(1)}, bf16[768]{0:T(1024)(128)(2,1)}, u32[]{:S(2)}) copy-start(bf16[768]{0:T(1024)(128)(2,1)} %param.35) | copy-start | bytes 4612
  103.4 5.1 %copy-start.14 = (bf16[3072]{0:T(1024)(128)(2,1)S(1)}, bf16[3072]{0:T(1024)(128)(2,1)}, u32[]{:S(2)}) copy-start(bf16[3072]{0:T(1024)(128)(2,1)} %param.38) | copy-start | bytes 18436
  103.4 5.2 %copy-start.17 = (bf16[768]{0:T(1024)(128)(2,1)S(1)}, bf16[768]{0:T(1024)(128)(2,1)}, u32[]{:S(2)}) copy-start(bf16[768]{0:T(1024)(128)(2,1)} %param.36) | copy-start | bytes 4612
  103.4 5.2 %copy-start.18 = (bf16[768]{0:T(1024)(128)(2,1)S(1)}, bf16[768]{0:T(1024)(128)(2,1)}, u32[]{:S(2)}) copy-start(bf16[768]{0:T(1024)(128)(2,1)} %param.40) | copy-start | bytes 4612
  103.4 5.2 %copy-start.19 = (bf16[768]{0:T(1024)(128)(2,1)S(1)}, bf16[768]{0:T(1024)(128)(2,1)}, u32[]{:S(2)}) copy-start(bf16[768]{0:T(1024)(128)(2,1)} %param.41) | copy-start | bytes 4612
  103.4 5.2 %copy-start.20 = (bf16[768]{0:T(1024)(128)(2,1)S(1)}, bf16[768]{0:T(1024)(128)(2,1)}, u32[]{:S(2)}) copy-start(bf16[768]{0:T(1024)(128)(2,1)} %param.42) | copy-start | bytes 4612
  103.4 30.8 %all-to-all-start = ((bf16[7,512,192]{2,0,1:T(8,128)(2,1)}), bf16[7,512,192]{2,0,1:T(8,128)(2,1)}, u32[]{:S(2)}, u32[]{:S(2)}) async-start(bf16[7,512,192]{2,0,1:T(8,128)(2,1)} %copy.98), calls=%async_computation | async-start | bytes 4194304 | tf_op jit(solution)/shard_map/all_to_all | solution.py:345
  137.7 1.8 copy-start.5
  139.5 1.5 copy-start.6
  141.0 67.4 %copy-start.2 = (f32[7,128,768]{2,1,0:T(8,128)}, f32[7,128,768]{2,1,0:T(8,128)S(1)}, u32[]{:S(2)}) copy-start(f32[7,128,768]{2,1,0:T(8,128)S(1)} %get-tuple-element.189) | copy-start | bytes 8257540
  141.1 37.2 %slice-start = ((s8[4718592]{0:T(1024)(128)(4,1)}), s8[4194304]{0:T(1024)(128)(4,1)S(1)}, s32[]{:S(2)}) async-start(s8[4718592]{0:T(1024)(128)(4,1)} %bitcast.217), calls=%async_computation.5 | async-start | bytes 8388608
  141.5 36.7 %slice-start.1 = ((s8[4718592]{0:T(1024)(128)(4,1)}), s8[524288]{0:T(1024)(128)(4,1)S(1)}, s32[]{:S(2)}) async-start(s8[4718592]{0:T(1024)(128)(4,1)} %bitcast.217), calls=%async_computation.6 | async-start | bytes 1048576
  178.2 4.8 copy-start.9
  183.1 1.3 copy-start.8
  187.9 11.0 %copy-start.11 = (bf16[7,128,768]{2,1,0:T(8,128)(2,1)}, bf16[7,128,768]{2,1,0:T(8,128)(2,1)S(1)}, u32[]{:S(2)}) copy-start(bf16[7,128,768]{2,1,0:T(8,128)(2,1)S(1)} %get-tuple-element.173) | copy-start | bytes 4128772
  208.4 1.5 copy-start.4
  209.9 1.1 copy-start.13
  216.2 24.5 %all-to-all-start.1 = ((bf16[7,128,768]{1,0,2:T(8,128)(2,1)}), bf16[7,128,768]{1,0,2:T(8,128)(2,1)}, u32[]{:S(2)}, u32[]{:S(2)}) async-start(bf16[7,128,768]{1,0,2:T(8,128)(2,1)} %copy.102), calls=%async_computation.1 | async-start | bytes 3145728 | tf_op jit(solution)/shard_map/all_to_all | solution.py:401
  220.6 267.0 %reduce-scatter.2.cloned.1.call-start = ((), (), s32[]{:S(2)}) async-start(), calls=%async_computation.4 | async-start | bytes 6881280 | tf_op jit(solution)/shard_map/reduce_scatter | solution.py:421
  251.7 70.4 %copy-start.23 = (bf16[768,192]{0,1:T(8,128)(2,1)S(1)}, bf16[768,192]{0,1:T(8,128)(2,1)}, u32[]{:S(2)}) copy-start(bf16[768,192]{0,1:T(8,128)(2,1)} %param.31) | copy-start | bytes 884740
  251.7 70.4 %copy-start.24 = (bf16[768,192]{0,1:T(8,128)(2,1)S(1)}, bf16[768,192]{0,1:T(8,128)(2,1)}, u32[]{:S(2)}) copy-start(bf16[768,192]{0,1:T(8,128)(2,1)} %param.30) | copy-start | bytes 884740
  251.7 70.4 %copy-start.25 = (bf16[768,192]{0,1:T(8,128)(2,1)S(1)}, bf16[768,192]{0,1:T(8,128)(2,1)}, u32[]{:S(2)}) copy-start(bf16[768,192]{0,1:T(8,128)(2,1)} %param.28) | copy-start | bytes 884740
  331.7 1.4 copy-start.7
  333.1 2.9 copy-start.12
  333.1 12.2 %slice-start.2 = ((s8[5505024]{0:T(1024)(128)(4,1)}), s8[4194304]{0:T(1024)(128)(4,1)S(1)}, s32[]{:S(2)}) async-start(s8[5505024]{0:T(1024)(128)(4,1)} %bitcast.219), calls=%async_computation.7 | async-start | bytes 8388608
  336.0 9.3 %copy-start.3 = (f32[7,128,768]{2,1,0:T(8,128)S(1)}, f32[7,128,768]{2,1,0:T(8,128)}, u32[]{:S(2)}) copy-start(f32[7,128,768]{2,1,0:T(8,128)} %copy-done.2) | copy-start | bytes 8257540
  336.0 9.3 %slice-start.3 = ((s8[5505024]{0:T(1024)(128)(4,1)}), s8[1310720]{0:T(1024)(128)(4,1)S(1)}, s32[]{:S(2)}) async-start(s8[5505024]{0:T(1024)(128)(4,1)} %bitcast.219), calls=%async_computation.8 | async-start | bytes 2621440
  372.7 5.3 %copy-start.10 = (bf16[7,512,3,64]{1,3,2,0:T(8,128)(2,1)S(1)}, bf16[7,512,3,64]{1,3,2,0:T(8,128)(2,1)}, u32[]{:S(2)}) copy-start(bf16[7,512,3,64]{1,3,2,0:T(8,128)(2,1)} %get-tuple-element.114) | copy-start | bytes 4128772
  486.8 5.4 %copy-start.1 = (bf16[768,768]{1,0:T(8,128)(2,1)S(1)}, bf16[768,768]{1,0:T(8,128)(2,1)}, u32[]{:S(2)}) copy-start(bf16[768,768]{1,0:T(8,128)(2,1)} %param.33) | copy-start | bytes 3538948
  (2 other events, 1.3 us)
Sparse Core Ops, SparseCore 0:
  9.6 44.6 all-gather.1
  331.9 53.1 reduce-scatter.1

commit v2 on v1

v2 whole, which is shorter than its diff:
```python
import functools

import jax
import jax.numpy as jnp
from jax import lax
from jax.experimental import pallas as pl
from jax.experimental.pallas import tpu as pltpu
from jax.sharding import PartitionSpec as P

HEAD_DIM = 64
EPSILON = 1e-12
MASKED = -1e30
SCALE = 0.125
F32, BF16 = jnp.float32, jnp.bfloat16
MIB = 1024 * 1024
NN, NT, TN = ((1,), (0,)), ((1,), (1,)), ((0,), (0,))
VMEM = pl.BlockSpec(memory_space=pltpu.VMEM)
SMEM = pl.BlockSpec(memory_space=pltpu.SMEM)
AHEAD = 7
LAG = (0, 2, 3, 4, 5)


def mesh_steps(sizes, axis):
    return [(axis, 1 << k) for k in range(sizes[axis].bit_length() - 1)]


def all_steps(sizes):
    head = mesh_steps(sizes, "head")
    return head[:1] + mesh_steps(sizes, "dp") + head[1:]


def bit_of(step):
    return lax.rem(lax.axis_index(step[0]) // step[1], 2)


def partner_of(step):
    return {step[0]: lax.axis_index(step[0]) + step[1] * (1 - 2 * bit_of(step))}


def chunk_order(sizes, steps):
    both = any(axis == "head" for axis, _ in steps)
    order = []
    for place in range(1 << len(steps)):
        at = {"dp": 0, "head": 0}
        for level, (axis, width) in enumerate(steps):
            if (place >> (len(steps) - 1 - level)) & 1:
                at[axis] += width
        order.append(at["dp"] * sizes["head"] + at["head"] if both else at["dp"])
    return order


def halves(step, count):
    bit = bit_of(step)
    return bit * (count // 2), (1 - bit) * (count // 2)


class Scatter:
    def __init__(self, steps, source, landing, send, recv, result):
        self.steps, self.source, self.landing = steps, source, landing
        self.send_sem, self.recv_sem, self.result = send, recv, result
        self.parts = source.shape[0]

    def held(self, level):
        return self.source if level == 0 else self.landing[level - 1]

    def copy(self, part, level):
        block = self.held(level)
        count = block.shape[1]
        _, other = halves(self.steps[level], count)
        return pltpu.make_async_remote_copy(
            src_ref=block.at[part, pl.ds(other, count // 2)],
            dst_ref=self.landing[level].at[part],
            send_sem=self.send_sem.at[part, level],
            recv_sem=self.recv_sem.at[part, level],
            device_id=partner_of(self.steps[level]),
            device_id_type=pl.DeviceIdType.MESH,
        )

    def start(self, part, level):
        self.copy(part, level).start()

    def land(self, part, level):
        self.copy(part, level).wait_recv()
        block, landed = self.held(level), self.landing[level]
        count = block.shape[1]
        mine, _ = halves(self.steps[level], count)
        last = level == len(self.steps) - 1

        def add(i, carry):
            total = landed[part, i].astype(jnp.float32) + block[part, mine + i].astype(jnp.float32)
            if last:
                self.result[part] = total
            else:
                landed[part, i] = total.astype(landed.dtype)
            return carry

        lax.fori_loop(0, count // 2, add, 0)

    def finish(self):
        for part in range(self.parts):
            for level in range(len(self.steps)):
                self.copy(part, level).wait_send()


class Everywhere:
    def __init__(self, steps, source, landing, total, send, recv, result):
        self.steps, self.source, self.landing, self.total = steps, source, landing, total
        self.send_sem, self.recv_sem, self.result = send, recv, result

    def held(self, level):
        return self.source if level == 0 else self.total.at[level - 1]

    def copy(self, level):
        return pltpu.make_async_remote_copy(
            src_ref=self.held(level),
            dst_ref=self.landing.at[level],
            send_sem=self.send_sem.at[level],
            recv_sem=self.recv_sem.at[level],
            device_id=partner_of(self.steps[level]),
            device_id_type=pl.DeviceIdType.MESH,
        )

    def land(self, level):
        self.copy(level).wait_recv()
        total = self.held(level)[...] + self.landing[level]
        if level == len(self.steps) - 1:
            self.result[...] = total
        else:
            self.total[level] = total

    def finish(self):
        for level in range(len(self.steps)):
            self.copy(level).wait_send()


def greet(steps):
    barrier = pltpu.get_barrier_semaphore()
    for step in steps:
        pl.semaphore_signal(
            barrier, inc=1, device_id=partner_of(step), device_id_type=pl.DeviceIdType.MESH
        )
    pl.semaphore_wait(barrier, len(steps))


def other_in_head(steps):
    index = lax.axis_index("head")
    for step in steps:
        index = index + step[1] * (1 - 2 * bit_of(step))
    return index


def greet_all(devices):
    barrier = pltpu.get_barrier_semaphore()
    for device in devices:
        pl.semaphore_signal(
            barrier, inc=1, device_id=device, device_id_type=pl.DeviceIdType.MESH
        )
    pl.semaphore_wait(barrier, len(devices))


def head_devices(steps):
    return [{"head": other_in_head(group)} for group in ([steps[0]], [steps[1]], steps)]


def send(src, dst, send_sem, recv_sem, device):
    return pltpu.make_async_remote_copy(
        src_ref=src,
        dst_ref=dst,
        send_sem=send_sem,
        recv_sem=recv_sem,
        device_id=device,
        device_id_type=pl.DeviceIdType.MESH,
    )


def dot(left, right, contract):
    return lax.dot_general(left, right, (contract, ((), ())), preferred_element_type=F32)


def fill_mask(length, mask):
    row = lax.broadcasted_iota(jnp.int32, mask.shape, 0)
    mask[...] = jnp.where(row < length, 0.0, MASKED)


def widen(tile, width):
    return jnp.concatenate([tile] * (width // tile.shape[1]), axis=1)


def attend_kernel(
    steps, x_ref, len_ref, w_ref, b_ref, rows_ref, qkv_ref, ctx_ref, lse_ref, tok_ref, mask, *sems
):
    groups, block, _ = x_ref.shape
    length = rows_ref.shape[1]
    width = w_ref.shape[0] // 3
    heads = width // HEAD_DIM
    me = lax.axis_index("head")
    near, far, across = head_devices(steps)
    far_send, far_recv, near_send, near_recv, relay_send, relay_recv, tok_send, tok_recv = sems

    def own(s, index):
        return rows_ref.at[s, pl.ds(pl.multiple_of(index * block, block), block)]

    def far_copy(s):
        return send(x_ref.at[s], own(s, me), far_send.at[s], far_recv.at[s], far)

    def near_copy(s):
        return send(x_ref.at[s], own(s, me), near_send.at[s], near_recv.at[s], near)

    def relay_copy(s):
        block_ref = own(s, far["head"])
        return send(block_ref, block_ref, relay_send.at[s], relay_recv.at[s], near)

    def token_copy(s, way):
        device = (near, far, across)[way]
        return send(
            ctx_ref.at[s, device["head"]],
            tok_ref.at[s, me],
            tok_send.at[s, way],
            tok_recv.at[s, way],
            device,
        )

    greet_all([near, far, across])
    ahead = min(AHEAD, groups)
    for s in range(ahead):
        far_copy(s).start()
        near_copy(s).start()

    def place(s, carry):
        rows_ref[s, pl.ds(pl.multiple_of(me * block, block), block)] = x_ref[s]
        return carry

    lax.fori_loop(0, groups, place, 0)
    far_copy(0).wait_recv()
    relay_copy(0).start()

    def sequence(s, carry):
        @pl.when(s + ahead < groups)
        def _():
            far_copy(s + ahead).start()
            near_copy(s + ahead).start()

        near_copy(s).wait_recv()
        relay_copy(s).wait_recv()
        fill_mask(len_ref[s], mask)
        made = dot(w_ref[...], rows_ref[s], NT) + widen(b_ref[...], length)
        qkv_ref[s, :width] = (made[:width].astype(BF16).astype(F32) * SCALE).astype(BF16)
        qkv_ref[s, width:] = made[width:].astype(BF16)
        for h in range(heads):
            at = h * HEAD_DIM
            q = qkv_ref[s, at : at + HEAD_DIM]
            k = qkv_ref[s, width + at : width + at + HEAD_DIM]
            v = qkv_ref[s, 2 * width + at : 2 * width + at + HEAD_DIM]
            scores = dot(k.T, q, NN) + widen(mask[...], length)
            top = jnp.max(scores, axis=0, keepdims=True)
            weights = jnp.exp(scores - top).astype(BF16)
            sums = dot(jnp.concatenate([v, jnp.ones((16, length), BF16)], axis=0), weights, NN)
            total = sums[HEAD_DIM : HEAD_DIM + 1]
            context = (sums[:HEAD_DIM] * (1.0 / total)).astype(BF16)
            for d in range(length // block):
                ctx_ref[s, d, at : at + HEAD_DIM] = context[:, d * block : (d + 1) * block]
            lse_ref[s, h : h + 1] = top + jnp.log(total)
            if h == 0:

                @pl.when(s + 1 < groups)
                def _():
                    far_copy(s + 1).wait_recv()
                    relay_copy(s + 1).start()

        tok_ref[s, me] = ctx_ref[s, me]
        for way in range(3):
            token_copy(s, way).start()
        return carry

    lax.fori_loop(0, groups, sequence, 0)

    def finish(s, carry):
        far_copy(s).wait_send()
        near_copy(s).wait_send()
        relay_copy(s).wait_send()
        for way in range(3):
            token_copy(s, way).wait()
        return carry

    lax.fori_loop(0, groups, finish, 0)


def attend_all(sizes, inputs, lengths, weight, bias):
    groups, block, model_width = inputs.shape
    length = block * sizes["head"]
    width = weight.shape[0] // 3
    dma = pltpu.SemaphoreType.DMA
    steps = mesh_steps(sizes, "head")
    shape = jax.ShapeDtypeStruct
    return pl.pallas_call(
        functools.partial(attend_kernel, steps),
        out_shape=[
            shape((groups, length, model_width), BF16),
            shape((groups, 3 * width, length), BF16),
            shape((groups, sizes["head"], width, block), BF16),
            shape((groups, width // HEAD_DIM, length), F32),
            shape((groups, sizes["head"], width, block), BF16),
        ],
        in_specs=[VMEM, SMEM, VMEM, VMEM],
        out_specs=[VMEM] * 5,
        scratch_shapes=[pltpu.VMEM((length, 128), F32)] + [dma((groups,))] * 6 + [dma((groups, 3))] * 2,
        compiler_params=pltpu.CompilerParams(
            collective_id=0, has_side_effects=True, vmem_limit_bytes=48 * MIB
        ),
    )(inputs, lengths, weight, bias)


def place_of(sizes, dp, head):
    at = head % 2
    for k in range(sizes["dp"].bit_length() - 1):
        at = at * 2 + (dp // (1 << k)) % 2
    return at * 2 + head // 2


def store_chunk(wide_ref, place, base, rows, values):
    unit = wide_ref.shape[2]
    at = 0
    while at < rows:
        part, low = divmod(base + at, unit)
        count = min(rows - at, unit - low)
        wide_ref[part, place, low : low + count] = values[at : at + count]
        at += count


def center(v):
    return v - jnp.mean(v, axis=-1, keepdims=True)


def dense_kernel(
    sizes,
    x_ref,
    tok_ref,
    cot_ref,
    wo_ref,
    w1_ref,
    w2_ref,
    b1_ref,
    vec_ref,
    out_ref,
    dsum_ref,
    dctx_ref,
    small_ref,
    wide_ref,
    active,
    slope,
    low_ref,
    upper,
    attended,
    context,
    normed,
    branch,
    inverse,
):
    tokens, model = x_ref.shape
    hidden = w1_ref.shape[1]
    groups, block = tok_ref.shape[0], tok_ref.shape[2]
    tile, tall = model, tokens // 2
    devices = sizes["dp"] * sizes["head"]
    output_bias, gain1, shift1, outer_bias, gain2, shift2 = [vec_ref[i : i + 1] for i in range(6)]

    def rows_of(i):
        return pl.ds(pl.multiple_of(i * tall, tall), tall)

    def columns_of(j):
        return pl.ds(pl.multiple_of(j * tile, tile), tile)

    def add_small(row, value):
        small_ref[pl.ds(row, 1)] = small_ref[pl.ds(row, 1)] + jnp.sum(value, axis=0, keepdims=True)

    small_ref[...] = jnp.zeros_like(small_ref)

    def turn(s, carry):
        context[pl.ds(pl.multiple_of(s * block, block), block)] = tok_ref[s].T
        return carry

    lax.fori_loop(0, groups, turn, 0)

    def project(i, carry):
        rows = rows_of(i)
        v = center(x_ref[rows].astype(F32) + dot(context[rows], wo_ref[...], NN) + output_bias)
        r = lax.rsqrt(jnp.mean(v * v, axis=-1, keepdims=True) + EPSILON)
        n = v * r
        normed[rows] = n
        inverse[rows] = r
        low_ref[rows] = (n * gain1 + shift1).astype(BF16)
        return carry

    lax.fori_loop(0, 2, project, 0)

    def forward(t, carry):
        rows, columns = rows_of(t % 2), columns_of(t // 2)
        h = dot(low_ref[rows], w1_ref[:, columns], NN) + b1_ref[:, columns]
        phi = 0.5 + 0.5 * lax.erf(h * 0.7071067811865476)
        a = (h * phi).astype(BF16)
        active[rows, columns] = a
        slope[rows, columns] = (phi + h * jnp.exp(-0.5 * h * h) * 0.3989422804014327).astype(BF16)
        made = dot(a, w2_ref[columns], NN)

        @pl.when(t < 2)
        def _():
            branch[rows] = made

        @pl.when(t >= 2)
        def _():
            branch[rows] = branch[rows] + made

        return carry

    lax.fori_loop(0, 2 * (hidden // tile), forward, 0)

    def second(i, carry):
        rows = rows_of(i)
        v = center(normed[rows] * gain1 + shift1 + branch[rows] + outer_bias)
        r = lax.rsqrt(jnp.mean(v * v, axis=-1, keepdims=True) + EPSILON)
        n = v * r
        out_ref[rows] = (n * gain2 + shift2).astype(BF16)
        g = cot_ref[rows].astype(F32)
        u = g * gain2
        d = r * (center(u) - n * jnp.mean(u * n, axis=-1, keepdims=True))
        branch[rows] = d
        d_low = d.astype(BF16)
        upper[rows] = d_low
        add_small(4, d_low.astype(F32))
        add_small(5, g * n)
        add_small(6, g)
        return carry

    lax.fori_loop(0, 2, second, 0)

    def backward(t, carry):
        j = t // 2
        rows, columns = rows_of(t % 2), columns_of(j)
        d = (dot(upper[rows], w2_ref[columns], NT) * slope[rows, columns].astype(F32)).astype(BF16)
        slope[rows, columns] = d
        add_small(8 + j, d.astype(F32))
        branch[rows] = branch[rows] + dot(d, w1_ref[:, columns], NT)
        return carry

    lax.fori_loop(0, 2 * (hidden // tile), backward, 0)

    def third(i, carry):
        rows = rows_of(i)
        d, n = branch[rows], normed[rows]
        u = d * gain1
        total = inverse[rows] * (center(u) - n * jnp.mean(u * n, axis=-1, keepdims=True))
        dsum_ref[rows] = total
        total_low = total.astype(BF16)
        attended[rows] = total_low
        add_small(0, total_low.astype(F32))
        add_small(1, d * n)
        add_small(2, d)
        return carry

    lax.fori_loop(0, 2, third, 0)

    def context_back(i, carry):
        rows = pl.ds(pl.multiple_of(i * 256, 256), 256)
        made = dot(wo_ref[rows], attended[...], NT).astype(BF16)
        for s in range(groups):
            dctx_ref[s, rows] = made[:, s * block : (s + 1) * block]
        return carry

    lax.fori_loop(0, model // 256, context_back, 0)

    per = hidden // devices
    each = tile // (per * sizes["head"])

    def gradients(j, carry):
        columns = columns_of(j)
        for base, left, right in ((0, active, upper), (per, slope, low_ref)):
            made = dot(left[:, columns], right[...], TN).astype(BF16)
            for q in range(tile // per):
                place = place_of(sizes, j * each + q // sizes["head"], q % sizes["head"])
                store_chunk(wide_ref, place, base, per, made[q * per : (q + 1) * per])
        return carry

    lax.fori_loop(0, hidden // tile, gradients, 0)
    made = dot(attended[...], context[...], TN).astype(BF16)
    per_out = model // devices
    for q in range(devices):
        place = place_of(sizes, q // sizes["head"], q % sizes["head"])
        store_chunk(wide_ref, place, 2 * per, per_out, made[q * per_out : (q + 1) * per_out])
    used = (2 * per + per_out) % wide_ref.shape[2]
    if used:
        spare = wide_ref.shape[2] - used

        def clear(place, carry):
            wide_ref[wide_ref.shape[0] - 1, place, used:] = jnp.zeros((spare, model), BF16)
            return carry

        lax.fori_loop(0, devices, clear, 0)


def dense_all(sizes, x, tok, cot, wo, w1, w2, b1, vec):
    tokens, model = x.shape
    hidden = w1.shape[1]
    groups, _, block = tok.shape
    devices = sizes["dp"] * sizes["head"]
    rows = round_up((2 * hidden + model) // devices, 32)
    shape = jax.ShapeDtypeStruct
    return pl.pallas_call(
        functools.partial(dense_kernel, sizes),
        out_shape=[
            shape((tokens, model), BF16),
            shape((tokens, model), F32),
            shape((groups, model, block), BF16),
            shape((8 + hidden // model, model), F32),
            shape((rows // 32, devices, 32, model), BF16),
        ],
        in_specs=[VMEM] * 8,
        out_specs=[VMEM] * 5,
        scratch_shapes=[pltpu.VMEM((tokens, hidden), BF16)] * 2
        + [pltpu.VMEM((tokens, model), BF16)] * 4
        + [pltpu.VMEM((tokens, model), F32)] * 2
        + [pltpu.VMEM((tokens, 1), F32)],
        compiler_params=pltpu.CompilerParams(vmem_limit_bytes=60 * MIB),
    )(x, tok, cot, wo, w1, w2, b1, vec)


def return_kernel(
    sizes,
    rows_ref,
    qkv_ref,
    ctx_ref,
    lse_ref,
    len_ref,
    dtok_ref,
    dsum_ref,
    w_ref,
    small_ref,
    wide_ref,
    dx_ref,
    wide_out,
    head_out,
    small_out,
    bias_out,
    mask,
    dctx,
    joint,
    dx_part,
    weight_sum,
    bias_sum,
    bias_full,
    near_buf,
    near_land,
    far_buf,
    far_land,
    head_src,
    *scratch,
):
    steps, dp_steps, head_steps = all_steps(sizes), mesh_steps(sizes, "dp"), mesh_steps(sizes, "head")
    count = len(steps)
    wide_land, scratch = scratch[:count], scratch[count:]
    head_land, scratch = scratch[: len(dp_steps)], scratch[len(dp_steps) :]
    small_land, small_total, bias_land, bias_total = scratch[:4]
    sems = scratch[4:]
    groups, length, model = rows_ref.shape
    width = w_ref.shape[0] // 3
    heads = width // HEAD_DIM
    block = length // sizes["head"]
    me = lax.axis_index("head")
    near, far, across = head_devices(head_steps)
    low_bit, high_bit = bit_of(head_steps[0]), bit_of(head_steps[1])
    wide = Scatter(steps, wide_ref, wide_land, sems[0], sems[1], wide_out)
    head = Scatter(dp_steps, head_src, head_land, sems[2], sems[3], head_out)
    small = Everywhere(steps, small_ref, small_land, small_total, sems[4], sems[5], small_out)
    biases = Everywhere(steps, bias_full, bias_land, bias_total, sems[6], sems[7], bias_out)
    tok_send, tok_recv, near_send, near_recv, far_send, far_recv = sems[8:]

    def token_copy(s, way):
        device = (near, far, across)[way]
        return send(
            dtok_ref.at[s, device["head"]],
            dctx.at[s, me],
            tok_send.at[s, way],
            tok_recv.at[s, way],
            device,
        )

    def near_copy(s):
        return send(near_buf.at[s % 2], near_land.at[s], near_send.at[s], near_recv.at[s], near)

    def far_copy(s):
        return send(far_buf.at[s], far_land.at[s], far_send.at[s], far_recv.at[s], far)

    greet_all([near, far, across] + [partner_of(step) for step in dp_steps])
    small.copy(0).start()

    def begin(s, carry):
        for way in range(3):
            token_copy(s, way).start()
        dctx[s, me] = dtok_ref[s, me]
        return carry

    lax.fori_loop(0, groups, begin, 0)

    def begin_wide(part, carry):
        wide.start(part, 0)
        return carry

    lax.fori_loop(0, wide.parts, begin_wide, 0)
    weight_sum[...] = jnp.zeros_like(weight_sum)
    bias_sum[...] = jnp.zeros_like(bias_sum)

    def wide_turn(t):
        for level in reversed(range(count)):
            part = t - LAG[min(level, len(LAG) - 1)] - max(0, level + 1 - len(LAG))

            def step(level=level, part=part):
                wide.land(part, level)
                if level + 1 < count:
                    wide.start(part, level + 1)

            if isinstance(t, int):
                if 0 <= part < wide.parts:
                    step()
            else:
                pl.when(jnp.logical_and(part >= 0, part < wide.parts))(step)

    def sequence(s, carry):
        for way in range(3):
            token_copy(s, way).wait_recv()
        fill_mask(len_ref[s], mask)
        for h in range(heads):
            at = h * HEAD_DIM
            q = qkv_ref[s, at : at + HEAD_DIM]
            k = qkv_ref[s, width + at : width + at + HEAD_DIM]
            v = qkv_ref[s, 2 * width + at : 2 * width + at + HEAD_DIM]
            part = slice(at, at + HEAD_DIM)
            upper = jnp.concatenate([dctx[s, d, part] for d in range(length // block)], axis=1)
            context = jnp.concatenate([ctx_ref[s, d, part] for d in range(length // block)], axis=1)
            delta = jnp.sum(upper.astype(F32) * context.astype(F32), axis=0, keepdims=True)
            scores = dot(k.T, q, NN) + widen(mask[...], length)
            weights = jnp.exp(scores - lse_ref[s, h : h + 1])
            d_weights = dot(v.T, upper, NN)
            d_scores = (weights * (d_weights - delta)).astype(BF16)
            joint[at : at + HEAD_DIM] = (dot(k, d_scores, NN) * SCALE).astype(BF16)
            joint[width + at : width + at + HEAD_DIM] = dot(q, d_scores, NT).astype(BF16)
            joint[2 * width + at : 2 * width + at + HEAD_DIM] = dot(
                upper, weights.astype(BF16), NT
            ).astype(BF16)
        dx_part[...] = dot(joint[...], w_ref[...], TN)

        @pl.when(s >= 2)
        def _():
            near_copy(s - 2).wait_send()

        for i in range(2):
            theirs = pl.ds(pl.multiple_of((2 * i + 1 - low_bit) * block, block), block)
            near_buf[s % 2, i] = dx_part[theirs].astype(BF16)
        near_copy(s).start()
        weight_sum[...] += dot(rows_ref[s], joint[...], ((0,), (1,)))
        bias_sum[...] += dot(jnp.ones((8, length), BF16), joint[...], NT)
        wide_turn(s)
        mine = pl.ds(pl.multiple_of((2 * high_bit + low_bit) * block, block), block)
        others = pl.ds(pl.multiple_of((2 * (1 - high_bit) + low_bit) * block, block), block)
        near_copy(s).wait_recv()
        far_buf[s] = (dx_part[others] + near_land[s, 1 - high_bit].astype(F32)).astype(BF16)
        far_copy(s).start()
        dx_ref[s] = dx_part[mine] + near_land[s, high_bit].astype(F32) + dsum_ref[s]

        @pl.when(s < count)
        def _():
            for level in range(count):

                @pl.when(s == level)
                def _():
                    small.land(level)
                    if level + 1 < count:
                        small.copy(level + 1).start()

        return carry

    lax.fori_loop(0, groups, sequence, 0)
    for level in range(groups, count):
        small.land(level)
        if level + 1 < count:
            small.copy(level + 1).start()
    unit = head_src.shape[2]
    rows = model // sizes["dp"]
    for dp in range(sizes["dp"]):
        place = 0
        for k in range(len(dp_steps)):
            place = place * 2 + (dp >> k) % 2
        store_chunk(head_src, place, 0, rows, weight_sum[dp * rows : (dp + 1) * rows].astype(BF16))
        if rows % unit:
            head_src[head_src.shape[0] - 1, place, rows % unit :] = jnp.zeros(
                (unit - rows % unit, 3 * width), BF16
            )
    bias_full[...] = jnp.zeros_like(bias_full)
    bias_full[pl.ds(me, 1)] = bias_sum[0:1]
    biases.copy(0).start()
    for part in range(head.parts):
        head.start(part, 0)
    last_turn = wide.parts + LAG[-1] + max(0, count - len(LAG))
    for t in range(max(last_turn - groups, head.parts + len(dp_steps) - 1, count)):
        for level in reversed(range(len(dp_steps))):
            part = t - level
            if 0 <= part < head.parts:
                head.land(part, level)
                if level + 1 < len(dp_steps):
                    head.start(part, level + 1)
        wide_turn(t + groups)
        if t < count:
            biases.land(t)
            if t + 1 < count:
                biases.copy(t + 1).start()

    def finish(s, carry):
        far_copy(s).wait_recv()
        dx_ref[s] = dx_ref[s] + far_land[s].astype(F32)
        far_copy(s).wait_send()
        for way in range(3):
            token_copy(s, way).wait_send()
        return carry

    lax.fori_loop(0, groups, finish, 0)
    for s in range(max(groups - 2, 0), groups):
        near_copy(s).wait_send()
    wide.finish()
    head.finish()
    small.finish()
    biases.finish()


def return_all(sizes, rows, qkv, ctx, lse, lengths, dtok, dsum, weight, small, wide):
    steps, dp_steps = all_steps(sizes), mesh_steps(sizes, "dp")
    count, dp_count = len(steps), len(dp_steps)
    groups, length, model = rows.shape
    block, joint_width = length // sizes["head"], weight.shape[0]
    head_rows = round_up(model // sizes["dp"], 16)
    unit = part_rows(head_rows)
    parts = head_rows // unit
    dma = pltpu.SemaphoreType.DMA
    shape = jax.ShapeDtypeStruct

    def landing(lead, n, tail, length):
        return [pltpu.VMEM((lead, n >> (level + 1)) + tail, BF16) for level in range(length)]

    return pl.pallas_call(
        functools.partial(return_kernel, sizes),
        out_shape=[
            shape((groups, block, model), F32),
            shape((wide.shape[0],) + wide.shape[2:], F32),
            shape((parts, unit, joint_width), F32),
            shape(small.shape, F32),
            shape((8, joint_width), F32),
        ],
        in_specs=[VMEM] * 4 + [SMEM] + [VMEM] * 5,
        out_specs=[VMEM] * 5,
        scratch_shapes=[
            pltpu.VMEM((length, 128), F32),
            pltpu.VMEM(dtok.shape, BF16),
            pltpu.VMEM((joint_width, length), BF16),
            pltpu.VMEM((length, model), F32),
            pltpu.VMEM((model, joint_width), F32),
            pltpu.VMEM((8, joint_width), F32),
            pltpu.VMEM((8, joint_width), F32),
            pltpu.VMEM((2, 2, block, model), BF16),
            pltpu.VMEM((groups, 2, block, model), BF16),
            pltpu.VMEM((groups, block, model), BF16),
            pltpu.VMEM((groups, block, model), BF16),
            pltpu.VMEM((parts, sizes["dp"], unit, joint_width), BF16),
        ]
        + landing(wide.shape[0], wide.shape[1], wide.shape[2:], count)
        + landing(parts, sizes["dp"], (unit, joint_width), dp_count)
        + [pltpu.VMEM((count,) + small.shape, F32)] * 2
        + [pltpu.VMEM((count, 8, joint_width), F32)] * 2
        + [dma((wide.shape[0], count))] * 2
        + [dma((parts, dp_count))] * 2
        + [dma((count,))] * 4
        + [dma((groups, 3))] * 2
        + [dma((groups,))] * 4,
        compiler_params=pltpu.CompilerParams(
            collective_id=1, has_side_effects=True, vmem_limit_bytes=60 * MIB
        ),
    )(rows, qkv, ctx, lse, lengths, dtok, dsum, weight, small, wide)


def round_up(value, unit):
    return -(-value // unit) * unit


def part_rows(rows):
    return 32 if rows % 32 == 0 else 16


def on_device(
    sizes,
    inputs,
    lengths,
    query_weight,
    query_bias,
    key_weight,
    value_weight,
    value_bias,
    attention_out_weight,
    output_bias,
    first_gain,
    first_shift,
    expand_weight,
    inner_bias,
    contract_weight,
    outer_bias,
    second_gain,
    second_shift,
    cotangent,
):
    groups, block, model = inputs.shape
    width = query_weight.shape[1]
    hidden = expand_weight.shape[1]
    devices = sizes["dp"] * sizes["head"]
    weight = jnp.concatenate([query_weight, key_weight, value_weight], axis=1).T
    bias = jnp.concatenate([query_bias, jnp.zeros_like(query_bias), value_bias]).astype(F32)
    bias = jnp.broadcast_to(bias[:, None], (3 * width, 128))
    rows, qkv, ctx, lse, tok = attend_all(sizes, inputs, lengths, weight, bias)
    zero = jnp.zeros_like(output_bias)
    vec = jnp.stack(
        [output_bias, first_gain, first_shift, outer_bias, second_gain, second_shift, zero, zero]
    ).astype(F32)
    output, dsum, dtok, small, wide = dense_all(
        sizes,
        inputs.reshape(groups * block, model),
        tok.reshape(groups, model, block),
        cotangent.reshape(groups * block, model),
        attention_out_weight,
        expand_weight,
        contract_weight,
        inner_bias.astype(F32)[None],
        vec,
    )
    dx, wide, head_part, small, biases = return_all(
        sizes,
        rows,
        qkv,
        ctx,
        lse,
        lengths,
        dtok.reshape(tok.shape),
        dsum.reshape(groups, block, model),
        weight,
        small,
        wide,
    )
    wide = wide.reshape(-1, model)
    inner, outer = hidden // devices, model // devices
    head_part = head_part.reshape(-1, 3 * width)[: model // sizes["dp"]]
    biases = biases[: sizes["head"]]
    return (
        output.reshape(inputs.shape),
        dx,
        head_part[:, :width],
        biases[:, :width].reshape(-1),
        head_part[:, width : 2 * width],
        head_part[:, 2 * width :],
        biases[:, 2 * width :].reshape(-1),
        wide[2 * inner : 2 * inner + outer].T,
        small[0],
        small[1],
        small[2],
        wide[inner : 2 * inner].T,
        small[8:].reshape(-1),
        wide[:inner],
        small[4],
        small[5],
        small[6],
    )


def solution(mesh):
    in_specs = (
        P("dp", "head", None),
        P("dp"),
        P(None, "head"),
        P("head"),
        P(None, "head"),
        P(None, "head"),
        P("head"),
        P(),
        P(),
        P(),
        P(),
        P(),
        P(),
        P(),
        P(),
        P(),
        P(),
        P("dp", "head", None),
    )
    out_specs = (
        P("dp", "head", None),
        P("dp", "head", None),
        P("dp", "head"),
        P(),
        P("dp", "head"),
        P("dp", "head"),
        P(),
        P(None, ("dp", "head")),
        P(),
        P(),
        P(),
        P(None, ("dp", "head")),
        P(),
        P(("dp", "head"), None),
        P(),
        P(),
        P(),
    )
    return jax.shard_map(
        functools.partial(on_device, dict(mesh.shape)), mesh=mesh, in_specs=in_specs, out_specs=out_specs, check_vma=False
    )
```

time: 505 us -> 260 us (0.51); the launches traced: 499 us -> 260 us
  matrix products: 175 us -> 0 us
  Pallas kernels: 95.2 us -> 234 us
  waiting for transfers between devices: 90.6 us -> 0 us
  other arithmetic: 58.1 us -> 3.86 us
  local copies, waits for them, and re-layouts: 55.8 us -> 21.1 us
  between operations: 15.2 us -> 0.75 us
  starting transfers between devices: 9.48 us -> 0 us
    dot_general x61 -> x0, matrix products: 175 us -> none  [the longest x14 26.1 us: masked_scores(): jnp.einsum('qhd,khd->hqk', queries, key_rows, preferred_element_type=jnp....]
    pallas_call x1 -> x3, Pallas kernels: 95.2 us -> 234 us  [the longest x1 122 us: return_all(): pl.pallas_call(functools.partial(return_kernel, sizes), out_shape=[shape(...]
    all_to_all x2 -> x0, waiting for transfers between devices: 45.7 us -> none  [the longest x1 25.6 us: on_device(): lax.all_to_all(context, 'head', split_axis=1, concat_axis=2, tiled=True)]
    all_gather x1 -> x0, waiting for transfers between devices: 44.3 us -> none  [on_device(): gathered_rows = lax.all_gather(inputs, 'head', axis=1, tiled=True)]
    convert_element_type x18 -> x2, other arithmetic: 35.2 us -> 1.36 us  [the longest x1 0.75 us: on_device(): jnp.concatenate([query_bias, jnp.zeros_like(query_bias), value_bias])]
    gather x3 -> x0, local copies, waits for them, and re-layouts: 16.6 us -> none  [pack_chunks(): joined = joined[np.array(chunk_order(sizes, steps))]]
    reduce_sum x14 -> x0, other arithmetic: 12.4 us -> none  [the longest x7 4.9 us: attend(): row_total = jnp.sum(exponent, axis=-1, keepdims=True)]
    reshape x5 -> x3, local copies, waits for them, and re-layouts: 13.4 us -> 1.95 us  [the longest x1 0.67 us: on_device(): biases[:, 2 * width:].reshape(-1)]
  transfers between devices with their start and end apart: 4 -> 0, of which waited for: 3 -> 0; matrix products, arithmetic and copies ran while one was open for 12% -> 0% of each run, Pallas kernels for 19% -> 0%
where the time goes in v2:
time: 260 us
  Pallas kernels  234 us (90%)
  local copies, waits for them, and re-layouts  21.1 us (8%)
  other arithmetic  3.86 us (1%)
    pallas_call x1, Pallas kernels, return_all(): pl.pallas_call(functools.partial(return_kernel, sizes), out_shape=[shape(...  122 us
    pallas_call x1, Pallas kernels, dense_all(): pl.pallas_call(functools.partial(dense_kernel, sizes), out_shape=[shape((...  58.6 us
    pallas_call x1, Pallas kernels, attend_all(): pl.pallas_call(functools.partial(attend_kernel, steps), out_shape=[shape(...  53.2 us
    unnamed x13, local copies, waits for them, and re-layouts  6.38 us

profile of v2, /device:TPU:0, one launch (start us, length us, event | category | flops | bytes accessed | tf_op | source)
XLA Modules:
  0.0 259.5 jit_solution(2396756172667447427)
XLA Ops:
  0.7 0.0 copy-start.5
  0.7 0.0 copy-start.1
  0.7 0.8 stack.24
  1.5 0.7 stack.25
  2.2 0.7 stack.26
  2.8 0.7 stack.27
  3.5 0.7 stack.28
  4.2 0.7 stack.29
  5.0 0.8 maximum_convert_fusion
  5.7 0.6 convert_element_type.12.vec_ref
  6.3 1.3 broadcast_in_dim.18
  7.6 0.1 broadcast_in_dim.15.b_ref
  7.7 1.2 maximum_bitcast_fusion.w_ref
  9.0 0.0 copy-done.5
  9.0 0.0 copy-done.1
  9.0 0.0 copy-start
  9.0 53.2 %shard_map.305 = (bf16[7,512,768]{2,1,0:T(8,128)(2,1)}, bf16[7,576,512]{2,1,0:T(8,128)(2,1)}, bf16[7,4,192,128]{3,2,1,0:T(8,128)(2,1)S(1)}, f32[7,3,512]{2,1,0:T(4,128)S(1)}, bf16[7,4,192,128]{3,2,1,0:T(8,128)(2,1)S(1)}) custom-call(bf16[7,128,768]{2,1,0:T(8,128)(2,1)S(1)} %copy-done.1, s32[7]{0:T(128)S(1)} %copy-done.5, ...), custom_call_target="tpu_custom_call" | custom-call | tf_op jit(solution)/shard_map/pallas_call | solution.py:295
  62.2 1.1 copy-done.2
  63.3 1.1 copy-done.3
  64.4 0.6 copy-done.4
  65.0 58.6 %shard_map.306 = (bf16[896,768]{1,0:T(8,128)(2,1)}, f32[896,768]{1,0:T(8,128)}, bf16[7,768,128]{2,1,0:T(8,128)(2,1)}, f32[12,768]{1,0:T(8,128)}, bf16[7,32,32,768]{3,2,1,0:T(8,128)(2,1)}) custom-call(bf16[896,768]{1,0:T(8,128)(2,1)} %bitcast.17, bf16[7,768,128]{2,1,0:T(8,128)(2,1)} %bitcast.18, bf16[896,768]{1,0:T(8,128)(2,1)} %bitcast.20, ...), custom_call_target="tpu_custom_call" | custom-call | tf_op jit(solution)/shard_map/pallas_call | solution.py:506
  123.7 122.0 %shard_map.307 = (f32[7,128,768]{2,1,0:T(8,128)}, f32[7,32,768]{2,1,0:T(8,128)}, f32[3,32,576]{2,1,0:T(8,128)}, f32[12,768]{1,0:T(8,128)}, f32[8,576]{1,0:T(8,128)}) custom-call(bf16[7,512,768]{2,1,0:T(8,128)(2,1)} %get-tuple-element.34.rows_ref, bf16[7,576,512]{2,1,0:T(8,128)(2,1)} %get-tuple-element.35.qkv_ref, bf16[7,4,192,128]{3,2,1,0:T(8,128)(2,1)} %copy-done.2, ...), custom_call_target="tpu_custom_call" | custom-call | tf_op jit(solution)/shard_map/pallas_call | solution.py:745
  245.6 0.7 fusion.2
  246.4 0.7 reshape.96
  247.0 0.7 reshape.95
  247.7 0.7 slice.65
  248.4 1.7 slice_reduce_fusion
  250.2 0.6 reshape.98
  250.8 1.8 fusion.1
  252.6 1.5 slice_bitcast_fusion
  254.1 1.9 fusion
  256.0 3.6 %copy.36 = f32[7,128,768]{2,1,0:T(8,128)} copy(f32[7,128,768]{2,1,0:T(8,128)} %get-tuple-element.78) | data formatting | bytes 5505024
  (7 shorter events, 0.1 us)
Async XLA Ops:
  0.7 8.3 %copy-start.5 = (s32[7]{0:T(128)S(1)}, s32[7]{0:T(128)}, u32[]{:S(2)}) copy-start(s32[7]{0:T(128)} %len_ref.3) | copy-start | bytes 88
  0.7 8.3 %copy-start.1 = (bf16[7,128,768]{2,1,0:T(8,128)(2,1)S(1)}, bf16[7,128,768]{2,1,0:T(8,128)(2,1)}, u32[]{:S(2)}) copy-start(bf16[7,128,768]{2,1,0:T(8,128)(2,1)} %x_ref.1) | copy-start | bytes 4128772
  9.0 114.7 %copy-start = (bf16[576,768]{1,0:T(8,128)(2,1)}, bf16[576,768]{1,0:T(8,128)(2,1)S(1)}, u32[]{:S(2)}) copy-start(bf16[576,768]{1,0:T(8,128)(2,1)S(1)} %maximum_bitcast_fusion.w_ref) | copy-start | bytes 2654212
  62.2 1.1 copy-start.2
  63.3 1.1 copy-start.3
  64.4 0.6 copy-start.4

commit v3 on v2

v3 whole, which is shorter than its diff:
```python
import functools

import jax
import jax.numpy as jnp
from jax import lax
from jax.experimental import pallas as pl
from jax.experimental.pallas import tpu as pltpu
from jax.sharding import PartitionSpec as P

HEAD_DIM = 64
EPSILON = 1e-12
MASKED = -1e30
SCALE = 0.125
F32, BF16 = jnp.float32, jnp.bfloat16
MIB = 1024 * 1024
NN, NT, TN = ((1,), (0,)), ((1,), (1,)), ((0,), (0,))
VMEM = pl.BlockSpec(memory_space=pltpu.VMEM)
SMEM = pl.BlockSpec(memory_space=pltpu.SMEM)
ANY = pl.BlockSpec(memory_space=pl.ANY)


def mesh_steps(sizes, axis):
    return [(axis, 1 << k) for k in range(sizes[axis].bit_length() - 1)]


def all_steps(sizes):
    head = mesh_steps(sizes, "head")
    return head[:1] + mesh_steps(sizes, "dp") + head[1:]


def bit_of(step):
    return lax.rem(lax.axis_index(step[0]) // step[1], 2)


def partner_of(step):
    return {step[0]: lax.axis_index(step[0]) + step[1] * (1 - 2 * bit_of(step))}


def halves(step, count):
    bit = bit_of(step)
    return bit * (count // 2), (1 - bit) * (count // 2)


class Scatter:
    def __init__(self, steps, source, landing, send, recv, result):
        self.steps, self.source, self.landing = steps, source, landing
        self.send_sem, self.recv_sem, self.result = send, recv, result
        self.parts = source.shape[0]

    def held(self, level):
        return self.source if level == 0 else self.landing[level - 1]

    def copy(self, part, level):
        block = self.held(level)
        count = block.shape[1]
        _, other = halves(self.steps[level], count)
        return pltpu.make_async_remote_copy(
            src_ref=block.at[part, pl.ds(other, count // 2)],
            dst_ref=self.landing[level].at[part],
            send_sem=self.send_sem.at[part, level],
            recv_sem=self.recv_sem.at[part, level],
            device_id=partner_of(self.steps[level]),
            device_id_type=pl.DeviceIdType.MESH,
        )

    def start(self, part, level):
        self.copy(part, level).start()

    def land(self, part, level):
        self.copy(part, level).wait_recv()
        block, landed = self.held(level), self.landing[level]
        count = block.shape[1]
        mine, _ = halves(self.steps[level], count)
        last = level == len(self.steps) - 1

        def add(i, carry):
            total = landed[part, i].astype(jnp.float32) + block[part, mine + i].astype(jnp.float32)
            if last:
                self.result[part] = total
            else:
                landed[part, i] = total.astype(landed.dtype)
            return carry

        lax.fori_loop(0, count // 2, add, 0)

    def finish(self):
        for part in range(self.parts):
            for level in range(len(self.steps)):
                self.copy(part, level).wait_send()


class Everywhere:
    def __init__(self, steps, source, landing, total, send, recv, result):
        self.steps, self.source, self.landing, self.total = steps, source, landing, total
        self.send_sem, self.recv_sem, self.result = send, recv, result

    def held(self, level):
        return self.source if level == 0 else self.total.at[level - 1]

    def copy(self, level):
        return pltpu.make_async_remote_copy(
            src_ref=self.held(level),
            dst_ref=self.landing.at[level],
            send_sem=self.send_sem.at[level],
            recv_sem=self.recv_sem.at[level],
            device_id=partner_of(self.steps[level]),
            device_id_type=pl.DeviceIdType.MESH,
        )

    def land(self, level):
        self.copy(level).wait_recv()
        total = self.held(level)[...] + self.landing[level]
        if level == len(self.steps) - 1:
            self.result[...] = total
        else:
            self.total[level] = total

    def finish(self):
        for level in range(len(self.steps)):
            self.copy(level).wait_send()


def other_in_head(steps):
    index = lax.axis_index("head")
    for step in steps:
        index = index + step[1] * (1 - 2 * bit_of(step))
    return index


def greet_all(devices):
    barrier = pltpu.get_barrier_semaphore()
    for device in devices:
        pl.semaphore_signal(
            barrier, inc=1, device_id=device, device_id_type=pl.DeviceIdType.MESH
        )
    pl.semaphore_wait(barrier, len(devices))


def head_devices(steps):
    return [{"head": other_in_head(group)} for group in ([steps[0]], [steps[1]], steps)]


def send(src, dst, send_sem, recv_sem, device):
    return pltpu.make_async_remote_copy(
        src_ref=src,
        dst_ref=dst,
        send_sem=send_sem,
        recv_sem=recv_sem,
        device_id=device,
        device_id_type=pl.DeviceIdType.MESH,
    )


def dot(left, right, contract):
    return lax.dot_general(left, right, (contract, ((), ())), preferred_element_type=F32)


def fill_mask(length, mask):
    row = lax.broadcasted_iota(jnp.int32, mask.shape, 0)
    mask[...] = jnp.where(row < length, 0.0, MASKED)


def widen(tile, width):
    return jnp.concatenate([tile] * (width // tile.shape[1]), axis=1)


class Layout:
    def __init__(self, sizes, hidden, model):
        devices = sizes["dp"] * sizes["head"]
        self.per, self.per_out = hidden // devices, model // devices
        self.pad = round_up(self.per, 16)
        self.slack = self.pad - self.per >= self.per_out
        self.out_pad = 0 if self.slack else round_up(self.per_out, 16)
        self.rows = 2 * self.pad + self.out_pad
        self.unit = 32 if self.pad % 32 == 0 and self.out_pad % 32 == 0 else 16
        self.parts = self.rows // self.unit
        self.in_tile = model // self.per
        self.tall = self.in_tile * self.pad
        self.out_at = self.pad + self.per if self.slack else 2 * self.pad
        self.arrays = [(0, self.pad), (self.pad, self.pad)] + (
            [] if self.slack else [(2 * self.pad, self.out_pad)]
        )


class Wide:
    def __init__(self, sizes, layout, steps, sources, landing, sems, result):
        self.sizes, self.layout, self.steps = sizes, layout, steps
        self.sources, self.landing, self.result = sources, landing, result
        self.first_send, self.first_recv, self.send_sem, self.recv_sem = sems

    def place(self, pair):
        dp, high = pair // 2, pair % 2
        at = 0
        for k in range(self.sizes["dp"].bit_length() - 1):
            at = at * 2 + (dp // (1 << k)) % 2
        return at * 2 + high

    def pair(self, place):
        rest, high = place // 2, place % 2
        dp = 0
        bits = self.sizes["dp"].bit_length() - 1
        for k in range(bits):
            dp = dp + ((rest // (1 << (bits - 1 - k))) % 2) * (1 << k)
        return dp * 2 + high

    def own(self, array, pair, bit, low, count):
        if array == 2:
            return self.sources[2].at[2 * pair + bit, pl.ds(low, count)]
        each = self.layout.in_tile // 2
        start = (2 * (pair % each) + bit) * self.layout.pad + low
        return self.sources[array].at[
            pair // each, pl.ds(pl.multiple_of(start, 16), count)
        ]

    def first(self, array, tile):
        base, rows = self.layout.arrays[array]
        bit = bit_of(self.steps[0])
        pairs = (
            range(self.sizes["dp"] * 2)
            if array == 2
            else range(tile * self.layout.in_tile // 2, (tile + 1) * self.layout.in_tile // 2)
        )
        for pair in pairs:
            send(
                self.own(array, pair, 1 - bit, 0, rows),
                self.landing[0].at[self.place(pair), pl.ds(base, rows)],
                self.first_send.at[array, tile],
                self.first_recv.at[array, tile],
                partner_of(self.steps[0]),
            ).start()

    def whole_first(self, array, tile):
        base, rows = self.layout.arrays[array]
        count = self.sizes["dp"] * 2 if array == 2 else self.layout.in_tile // 2
        ref = self.landing[0].at[pl.ds(0, count), pl.ds(base, rows)]
        return send(
            ref,
            ref,
            self.first_send.at[array, tile],
            self.first_recv.at[array, tile],
            partner_of(self.steps[0]),
        )

    def rows_of(self, part):
        return pl.ds(pl.multiple_of(part * self.layout.unit, 16), self.layout.unit)

    def land_first(self, array, tiles):
        for tile in range(tiles):
            self.whole_first(array, tile).wait_recv()
        base, rows = self.layout.arrays[array]
        unit = self.layout.unit
        bit = bit_of(self.steps[0])
        for low in range(0, rows, unit):
            at = pl.ds(base + low, unit)

            def add(place, carry, low=low, at=at):
                mine = self.own(array, self.pair(place), bit, low, unit)[...]
                total = self.landing[0][place, at].astype(F32) + mine.astype(F32)
                self.landing[0][place, at] = total.astype(BF16)
                return carry

            lax.fori_loop(0, self.landing[0].shape[0], add, 0)
            self.copy((base + low) // unit, 1).start()

    def copy(self, part, level):
        block = self.landing[level - 1]
        count = block.shape[0]
        _, other = halves(self.steps[level], count)
        return send(
            block.at[pl.ds(other, count // 2), self.rows_of(part)],
            self.landing[level].at[pl.ds(0, count // 2), self.rows_of(part)],
            self.send_sem.at[part, level],
            self.recv_sem.at[part, level],
            partner_of(self.steps[level]),
        )

    def land(self, part, level):
        self.copy(part, level).wait_recv()
        block, landed = self.landing[level - 1], self.landing[level]
        count = block.shape[0]
        mine, _ = halves(self.steps[level], count)
        rows = self.rows_of(part)
        last = level == len(self.steps) - 1

        def add(i, carry):
            total = landed[i, rows].astype(F32) + block[mine + i, rows].astype(F32)
            if last:
                self.result[rows] = total
            else:
                landed[i, rows] = total.astype(BF16)
            return carry

        lax.fori_loop(0, count // 2, add, 0)
        if not last:
            self.copy(part, level + 1).start()

    def turn(self, t):
        for level in reversed(range(1, len(self.steps))):
            part = t - (level - 1)
            if isinstance(t, int):
                if 0 <= part < self.layout.parts:
                    self.land(part, level)
            else:
                pl.when(jnp.logical_and(part >= 0, part < self.layout.parts))(
                    functools.partial(self.land, part, level)
                )

    def finish(self, tiles):
        for array in range(len(self.layout.arrays)):
            for tile in range(1 if array == 2 else tiles):
                self.whole_first(array, tile).wait_send()

        def done(part, carry):
            for level in range(1, len(self.steps)):
                self.copy(part, level).wait_send()
            return carry

        lax.fori_loop(0, self.layout.parts, done, 0)


def vector(vec_ref, model, index):
    return vec_ref[:, index * model : (index + 1) * model]


def attend_kernel(
    steps,
    x_ref,
    len_ref,
    wq_ref,
    wk_ref,
    wv_ref,
    vec_ref,
    rows_out,
    qkv_out,
    ctx_out,
    lse_ref,
    tok_out,
    rows_ref,
    qkv_ref,
    ctx_ref,
    w_ref,
    b_ref,
    mask,
    *sems,
):
    groups, block, _ = x_ref.shape
    length = rows_ref.shape[1]
    width = wq_ref.shape[0]
    heads = width // HEAD_DIM
    me = lax.axis_index("head")
    near, far, across = head_devices(steps)
    far_send, far_recv, near_send, near_recv, relay_send, relay_recv, tok_send, tok_recv = sems[:8]
    own_sem, rows_sem, qkv_sem, ctx_sem, mine_sem = sems[8:]

    def own(s, index):
        return rows_ref.at[s, pl.ds(pl.multiple_of(index * block, block), block)]

    def far_copy(s):
        return send(x_ref.at[s], own(s, me), far_send.at[s], far_recv.at[s], far)

    def near_copy(s):
        return send(x_ref.at[s], own(s, me), near_send.at[s], near_recv.at[s], near)

    def relay_copy(s):
        block_ref = own(s, far["head"])
        return send(block_ref, block_ref, relay_send.at[s], relay_recv.at[s], near)

    def token_copy(s, way):
        device = (near, far, across)[way]
        return send(
            ctx_ref.at[s, device["head"]],
            tok_out.at[s, me],
            tok_send.at[s, way],
            tok_recv.at[s, way],
            device,
        )

    def own_copy(s):
        return pltpu.make_async_copy(x_ref.at[s], own(s, me), own_sem.at[s])

    def rows_copy(s):
        return pltpu.make_async_copy(rows_ref.at[s], rows_out.at[s], rows_sem.at[s])

    def qkv_copy(s):
        return pltpu.make_async_copy(qkv_ref.at[s], qkv_out.at[s], qkv_sem.at[s])

    def ctx_copy(s):
        return pltpu.make_async_copy(ctx_ref.at[s], ctx_out.at[s], ctx_sem.at[s])

    def mine_copy(s):
        return pltpu.make_async_copy(ctx_ref.at[s, me], tok_out.at[s, me], mine_sem.at[s])

    greet_all([near, far, across])
    for s in range(groups):
        far_copy(s).start()
        near_copy(s).start()
        own_copy(s).start()
    w_ref[:width] = wq_ref[...]
    w_ref[width : 2 * width] = wk_ref[...]
    w_ref[2 * width :] = wv_ref[...]
    at = vec_ref.shape[1] - 2 * width
    b_ref[:width] = jnp.broadcast_to(vec_ref[:, at : at + width], (128, width)).T
    b_ref[width : 2 * width] = jnp.zeros((width, 128), F32)
    b_ref[2 * width :] = jnp.broadcast_to(vec_ref[:, at + width :], (128, width)).T
    far_copy(0).wait_recv()
    relay_copy(0).start()

    def sequence(s, carry):
        own_copy(s).wait()
        near_copy(s).wait_recv()
        relay_copy(s).wait_recv()
        rows_copy(s).start()
        fill_mask(len_ref[s], mask)
        made = dot(w_ref[...], rows_ref[s], NT) + widen(b_ref[...], length)
        qkv_ref[s, :width] = (made[:width].astype(BF16).astype(F32) * SCALE).astype(BF16)
        qkv_ref[s, width:] = made[width:].astype(BF16)
        qkv_copy(s).start()
        for h in range(heads):
            at = h * HEAD_DIM
            q = qkv_ref[s, at : at + HEAD_DIM]
            k = qkv_ref[s, width + at : width + at + HEAD_DIM]
            v = qkv_ref[s, 2 * width + at : 2 * width + at + HEAD_DIM]
            scores = dot(k.T, q, NN) + widen(mask[...], length)
            top = jnp.max(scores, axis=0, keepdims=True)
            weights = jnp.exp(scores - top).astype(BF16)
            sums = dot(jnp.concatenate([v, jnp.ones((16, length), BF16)], axis=0), weights, NN)
            total = sums[HEAD_DIM : HEAD_DIM + 1]
            context = (sums[:HEAD_DIM] * (1.0 / total)).astype(BF16)
            for d in range(length // block):
                ctx_ref[s, d, at : at + HEAD_DIM] = context[:, d * block : (d + 1) * block]
            lse_ref[s, h : h + 1] = top + jnp.log(total)
            if h == 0:

                @pl.when(s + 1 < groups)
                def _():
                    far_copy(s + 1).wait_recv()
                    relay_copy(s + 1).start()

        for way in range(3):
            token_copy(s, way).start()
        mine_copy(s).start()
        ctx_copy(s).start()
        return carry

    lax.fori_loop(0, groups, sequence, 0)

    def finish(s, carry):
        far_copy(s).wait_send()
        near_copy(s).wait_send()
        relay_copy(s).wait_send()
        rows_copy(s).wait()
        qkv_copy(s).wait()
        ctx_copy(s).wait()
        mine_copy(s).wait()
        for way in range(3):
            token_copy(s, way).wait()
        return carry

    lax.fori_loop(0, groups, finish, 0)


def attend_all(sizes, inputs, lengths, weights, vec):
    groups, block, model = inputs.shape
    length = block * sizes["head"]
    width = weights[0].shape[0]
    dma = pltpu.SemaphoreType.DMA
    steps = mesh_steps(sizes, "head")
    shape = jax.ShapeDtypeStruct
    blocks = (groups, sizes["head"], width, block)
    return pl.pallas_call(
        functools.partial(attend_kernel, steps),
        out_shape=[
            shape((groups, length, model), BF16),
            shape((groups, 3 * width, length), BF16),
            shape(blocks, BF16),
            shape((groups, width // HEAD_DIM, length), F32),
            shape(blocks, BF16),
        ],
        in_specs=[ANY, SMEM, VMEM, VMEM, VMEM, VMEM],
        out_specs=[ANY, ANY, ANY, VMEM, ANY],
        scratch_shapes=[
            pltpu.VMEM((groups, length, model), BF16),
            pltpu.VMEM((groups, 3 * width, length), BF16),
            pltpu.VMEM(blocks, BF16),
            pltpu.VMEM((3 * width, model), BF16),
            pltpu.VMEM((3 * width, 128), F32),
            pltpu.VMEM((length, 128), F32),
        ]
        + [dma((groups,))] * 6
        + [dma((groups, 3))] * 2
        + [dma((groups,))] * 5,
        compiler_params=pltpu.CompilerParams(
            collective_id=0, has_side_effects=True, vmem_limit_bytes=58 * MIB
        ),
    )(inputs, lengths, *weights, vec)


def center(v):
    return v - jnp.mean(v, axis=-1, keepdims=True)


def block_kernel(
    sizes,
    layout,
    x_ref,
    tok_ref,
    cot_ref,
    wo_ref,
    w1_ref,
    w2_ref,
    vec_ref,
    rows_ref,
    qkv_ref,
    ctx_ref,
    lse_ref,
    len_ref,
    wq_ref,
    wk_ref,
    wv_ref,
    out_ref,
    dx_ref,
    wide_out,
    head_out,
    small_out,
    bias_out,
    active,
    slope,
    out_grad,
    slots,
    wo,
    low_ref,
    upper,
    attended,
    context,
    normed,
    branch,
    inverse,
    tok,
    cot,
    small_in,
    mask,
    dctx,
    weight_sum,
    bias_sum,
    bias_full,
    w_ref,
    qkv_slots,
    ctx_slots,
    near_land,
    far_land,
    head_src,
    *scratch,
):
    steps, dp_steps, head_steps = all_steps(sizes), mesh_steps(sizes, "dp"), mesh_steps(sizes, "head")
    count = len(steps)
    wide_land, scratch = scratch[:count], scratch[count:]
    head_land, scratch = scratch[: len(dp_steps)], scratch[len(dp_steps) :]
    small_land, small_total, bias_land, bias_total = scratch[:4]
    sems = scratch[4:]
    groups, length, model = rows_ref.shape
    hidden = w1_ref.shape[1]
    width = wq_ref.shape[0]
    heads = width // HEAD_DIM
    block = length // sizes["head"]
    tokens = groups * block
    half = tokens // 2
    tiles = hidden // model
    me = lax.axis_index("head")
    near, far, across = head_devices(head_steps)
    low_bit, high_bit = bit_of(head_steps[0]), bit_of(head_steps[1])
    wide = Wide(sizes, layout, steps, [active, slope, out_grad], wide_land, sems[:4], wide_out)
    head = Scatter(dp_steps, head_src, head_land, sems[4], sems[5], head_out)
    small = Everywhere(steps, small_in, small_land, small_total, sems[6], sems[7], small_out)
    biases = Everywhere(steps, bias_full, bias_land, bias_total, sems[8], sems[9], bias_out)
    tok_send, tok_recv, near_send, near_recv, far_send, far_recv = sems[10:16]
    load_sem, slot_sem, seq_sem, out_sem, dx_sem = sems[16:]
    dx_part = normed

    output_bias, gain1, shift1, outer_bias, gain2, shift2 = [
        vector(vec_ref, model, i) for i in range(6)
    ]

    def token_copy(s, way):
        device = (near, far, across)[way]
        return send(
            tok.at[s, device["head"]],
            dctx.at[s, me],
            tok_send.at[s, way],
            tok_recv.at[s, way],
            device,
        )

    def near_buf(s):
        return slots.at[s % 2, 1, pl.ds(0, 2 * block)]

    def far_buf(s):
        return slots.at[s % 2, 1, pl.ds(2 * block, block)]

    def near_copy(s):
        return send(near_buf(s), near_land.at[s % 2], near_send.at[s], near_recv.at[s], near)

    def far_copy(s):
        return send(far_buf(s), far_land.at[s % 2], far_send.at[s], far_recv.at[s], far)

    loads = [
        pltpu.make_async_copy(src, dst, load_sem.at[i])
        for i, (src, dst) in enumerate(
            [
                (tok_ref, tok),
                (x_ref, upper),
                (wo_ref, wo),
                (cot_ref, cot),
                (wq_ref, w_ref.at[pl.ds(0, width)]),
                (wk_ref, w_ref.at[pl.ds(width, width)]),
                (wv_ref, w_ref.at[pl.ds(2 * width, width)]),
            ]
        )
    ]

    def slot_load(j, slot):
        columns = pl.ds(pl.multiple_of(j * model, model), model)
        return [
            pltpu.make_async_copy(w1_ref.at[:, columns], slots.at[slot, 0], slot_sem.at[slot, 0]),
            pltpu.make_async_copy(w2_ref.at[columns], slots.at[slot, 1], slot_sem.at[slot, 1]),
        ]

    def sequence_load(s):
        slot = s % 2
        return [
            pltpu.make_async_copy(
                rows_ref.at[s], slots.at[slot, 0, pl.ds(0, length)], seq_sem.at[slot, 0]
            ),
            pltpu.make_async_copy(qkv_ref.at[s], qkv_slots.at[slot], seq_sem.at[slot, 1]),
            pltpu.make_async_copy(ctx_ref.at[s], ctx_slots.at[slot], seq_sem.at[slot, 2]),
        ]

    def start(copies):
        for copy in copies:
            copy.start()

    def wait(copies):
        for copy in copies:
            copy.wait()

    start(loads)
    start(slot_load(0, 0))
    greet_all([near, far, across] + [partner_of(step) for step in dp_steps])

    def rows_at(i):
        return pl.ds(pl.multiple_of(i * half, half), half)

    def block_rows(s):
        return pl.ds(pl.multiple_of(s * block, block), block)

    def add_small(row, value):
        small_in[pl.ds(row, 1)] = small_in[pl.ds(row, 1)] + jnp.sum(value, axis=0, keepdims=True)

    small_in[...] = jnp.zeros_like(small_in)
    weight_sum[...] = jnp.zeros_like(weight_sum)
    bias_sum[...] = jnp.zeros_like(bias_sum)
    loads[0].wait()

    def turn(s, carry):
        context[block_rows(s)] = tok[s].reshape(model, block).T
        return carry

    lax.fori_loop(0, groups, turn, 0)
    wait(loads[1:])

    def project(i, carry):
        rows = rows_at(i)
        v = center(upper[rows].astype(F32) + dot(context[rows], wo[...], NN) + output_bias)
        r = lax.rsqrt(jnp.mean(v * v, axis=-1, keepdims=True) + EPSILON)
        n = v * r
        normed[rows] = n
        inverse[rows] = r
        low_ref[rows] = (n * gain1 + shift1).astype(BF16)
        return carry

    lax.fori_loop(0, 2, project, 0)

    def forward(j, carry):
        slot = j % 2
        wait(slot_load(j, slot))

        @pl.when(j + 1 < tiles)
        def _():
            start(slot_load(j + 1, 1 - slot))

        bias = vec_ref[:, pl.ds(pl.multiple_of((6 + j) * model, model), model)]
        for i in range(2):
            rows = pl.ds(i * half, half)
            h = dot(low_ref[rows], slots[slot, 0], NN) + bias
            phi = 0.5 + 0.5 * lax.erf(h * 0.7071067811865476)
            a = (h * phi).astype(BF16)
            active[j, rows] = a
            slope[j, rows] = (phi + h * jnp.exp(-0.5 * h * h) * 0.3989422804014327).astype(BF16)
            made = dot(a, slots[slot, 1], NN)

            @pl.when(j == 0)
            def _():
                branch[rows] = made

            @pl.when(j > 0)
            def _():
                branch[rows] = branch[rows] + made

        return carry

    lax.fori_loop(0, tiles, forward, 0)

    def second(i, carry):
        rows = rows_at(i)
        v = center(normed[rows] * gain1 + shift1 + branch[rows] + outer_bias)
        r = lax.rsqrt(jnp.mean(v * v, axis=-1, keepdims=True) + EPSILON)
        n = v * r
        g = cot[rows].astype(F32)
        u = g * gain2
        d = r * (center(u) - n * jnp.mean(u * n, axis=-1, keepdims=True))
        branch[rows] = d
        d_low = d.astype(BF16)
        upper[rows] = d_low
        cot[rows] = (n * gain2 + shift2).astype(BF16)
        add_small(4, d_low.astype(F32))
        add_small(5, g * n)
        add_small(6, g)
        return carry

    lax.fori_loop(0, 2, second, 0)
    out_copy = pltpu.make_async_copy(cot, out_ref, out_sem)
    out_copy.start()

    def put_chunks(array, tile, made):
        if layout.per == layout.pad:
            array[tile, : layout.tall] = made
        else:
            for q in range(layout.in_tile):
                array[tile, q * layout.pad : q * layout.pad + layout.per] = made[
                    q * layout.per : (q + 1) * layout.per
                ]

    for tile in range(tiles):
        put_chunks(active, tile, dot(active[tile, :tokens], upper[...], TN).astype(BF16))
        wide.first(0, tile)

    def backward(t, carry):
        j = tiles - 1 - t
        slot = j % 2

        @pl.when(t >= 2)
        def _():
            wait(slot_load(j, slot))

        for i in range(2):
            rows = pl.ds(i * half, half)
            d = (dot(upper[rows], slots[slot, 1], NT) * slope[j, rows].astype(F32)).astype(BF16)
            slope[j, rows] = d
            add_small(8 + j, d.astype(F32))
            branch[rows] = branch[rows] + dot(d, slots[slot, 0], NT)

        @pl.when(j >= 2)
        def _():
            start(slot_load(j - 2, slot))

        return carry

    backward(0, 0)
    wide.land_first(0, tiles)
    lax.fori_loop(1, tiles, backward, 0)
    start(sequence_load(0))

    def third(i, carry):
        rows = rows_at(i)
        d, n = branch[rows], normed[rows]
        u = d * gain1
        total = inverse[rows] * (center(u) - n * jnp.mean(u * n, axis=-1, keepdims=True))
        branch[rows] = total
        total_low = total.astype(BF16)
        attended[rows] = total_low
        add_small(0, total_low.astype(F32))
        add_small(1, d * n)
        add_small(2, d)
        return carry

    lax.fori_loop(0, 2, third, 0)
    small.copy(0).start()

    def context_back(h, carry):
        rows = pl.ds(pl.multiple_of(h * width, 16), width)
        made = dot(wo[rows], attended[...], NT).astype(BF16)
        for s in range(groups):
            tok[s, h] = made[:, s * block : (s + 1) * block]
        return carry

    lax.fori_loop(0, sizes["head"], context_back, 0)

    def begin(s, carry):
        for way in range(3):
            token_copy(s, way).start()
        dctx[s, me] = tok[s, me]
        return carry

    lax.fori_loop(0, groups, begin, 0)
    made_out = dot(attended[...], context[...], TN).astype(BF16)
    per_out = layout.per_out
    for tile in range(tiles):
        put_chunks(slope, tile, dot(slope[tile, :tokens], low_ref[...], TN).astype(BF16))
        if layout.slack:
            for q in range(layout.in_tile):
                chunk = tile * layout.in_tile + q
                at = q * layout.pad + layout.per
                slope[tile, at : at + per_out] = made_out[chunk * per_out : (chunk + 1) * per_out]
        wide.first(1, tile)
    if not layout.slack:
        for chunk in range(sizes["dp"] * sizes["head"]):
            out_grad[chunk, :per_out] = made_out[chunk * per_out : (chunk + 1) * per_out]
        wide.first(2, 0)

    def sequence(s, carry):
        slot = s % 2
        for way in range(3):
            token_copy(s, way).wait_recv()
        wait(sequence_load(s))

        @pl.when(s + 1 < groups)
        def _():
            start(sequence_load(s + 1))

        fill_mask(len_ref[s], mask)
        for h in range(heads):
            at = h * HEAD_DIM
            q = qkv_slots[slot, at : at + HEAD_DIM]
            k = qkv_slots[slot, width + at : width + at + HEAD_DIM]
            v = qkv_slots[slot, 2 * width + at : 2 * width + at + HEAD_DIM]
            part = slice(at, at + HEAD_DIM)
            d_ctx = jnp.concatenate([dctx[s, d, part] for d in range(length // block)], axis=1)
            ctx = jnp.concatenate([ctx_slots[slot, d, part] for d in range(length // block)], axis=1)
            delta = jnp.sum(d_ctx.astype(F32) * ctx.astype(F32), axis=0, keepdims=True)
            scores = dot(k.T, q, NN) + widen(mask[...], length)
            weights = jnp.exp(scores - lse_ref[s, h : h + 1])
            d_weights = dot(v.T, d_ctx, NN)
            d_scores = (weights * (d_weights - delta)).astype(BF16)
            qkv_slots[slot, at : at + HEAD_DIM] = (dot(k, d_scores, NN) * SCALE).astype(BF16)
            qkv_slots[slot, width + at : width + at + HEAD_DIM] = dot(q, d_scores, NT).astype(BF16)
            qkv_slots[slot, 2 * width + at : 2 * width + at + HEAD_DIM] = dot(
                d_ctx, weights.astype(BF16), NT
            ).astype(BF16)
        dx_part[:length] = dot(qkv_slots[slot], w_ref[...], TN)

        @pl.when(s >= 2)
        def _():
            near_copy(s - 2).wait_send()

        for i in range(2):
            theirs = pl.ds(pl.multiple_of((2 * i + 1 - low_bit) * block, block), block)
            slots[slot, 1, i * block : (i + 1) * block] = dx_part[theirs].astype(BF16)
        near_copy(s).start()
        weight_sum[...] += dot(slots[slot, 0, :length], qkv_slots[slot], ((0,), (1,)))
        bias_sum[...] += dot(jnp.ones((8, length), BF16), qkv_slots[slot], NT)

        @pl.when(s == 0)
        def _():
            wide.land_first(1, tiles)
            if not layout.slack:
                wide.land_first(2, 1)

        wide.turn(s)

        @pl.when(s >= 1)
        def _():
            far_copy(s - 1).wait_recv()
            rows = block_rows(s - 1)
            branch[rows] = branch[rows] + far_land[(s - 1) % 2].astype(F32)
            dx_copy(s - 1).start()

        @pl.when(s >= 2)
        def _():
            far_copy(s - 2).wait_send()

        mine = pl.ds(pl.multiple_of((2 * high_bit + low_bit) * block, block), block)
        others = pl.ds(pl.multiple_of((2 * (1 - high_bit) + low_bit) * block, block), block)
        near_copy(s).wait_recv()
        landed_mine = near_land[slot, pl.ds(pl.multiple_of(high_bit * block, block), block)]
        landed_other = near_land[slot, pl.ds(pl.multiple_of((1 - high_bit) * block, block), block)]
        slots[slot, 1, 2 * block : 3 * block] = (dx_part[others] + landed_other.astype(F32)).astype(BF16)
        far_copy(s).start()
        rows = block_rows(s)
        branch[rows] = branch[rows] + dx_part[mine] + landed_mine.astype(F32)
        for level in range(count):

            @pl.when(s == level)
            def _():
                small.land(level)
                if level + 1 < count:
                    small.copy(level + 1).start()

        return carry

    def dx_copy(s):
        return pltpu.make_async_copy(branch.at[block_rows(s)], dx_ref.at[block_rows(s)], dx_sem.at[s])

    lax.fori_loop(0, groups, sequence, 0)
    for level in range(groups, count):
        small.land(level)
        if level + 1 < count:
            small.copy(level + 1).start()
    unit = head_src.shape[2]
    rows = model // sizes["dp"]
    for dp in range(sizes["dp"]):
        place = 0
        for k in range(len(dp_steps)):
            place = place * 2 + (dp >> k) % 2
        store_chunk(head_src, place, 0, rows, weight_sum[dp * rows : (dp + 1) * rows].astype(BF16))
        if rows % unit:
            head_src[head_src.shape[0] - 1, place, rows % unit :] = jnp.zeros(
                (unit - rows % unit, 3 * width), BF16
            )
    for part in range(head.parts):
        head.start(part, 0)
    bias_full[...] = jnp.zeros_like(bias_full)
    bias_full[pl.ds(me, 1)] = bias_sum[0:1]
    biases.copy(0).start()
    last = groups - 1
    far_copy(last).wait_recv()
    branch[last * block :] = branch[last * block :] + far_land[last % 2].astype(F32)
    dx_copy(last).start()
    last_turn = layout.parts + count - 2
    for t in range(max(last_turn - groups, head.parts + len(dp_steps) - 1, count)):
        wide.turn(t + groups)
        for level in reversed(range(len(dp_steps))):
            part = t - level
            if 0 <= part < head.parts:
                head.land(part, level)
                if level + 1 < len(dp_steps):
                    head.start(part, level + 1)
        if t < count:
            biases.land(t)
            if t + 1 < count:
                biases.copy(t + 1).start()

    def finish(s, carry):
        dx_copy(s).wait()
        for way in range(3):
            token_copy(s, way).wait_send()
        return carry

    lax.fori_loop(0, groups, finish, 0)
    for s in range(max(groups - 2, 0), groups):
        near_copy(s).wait_send()
        far_copy(s).wait_send()
    out_copy.wait()
    wide.finish(tiles)
    head.finish()
    small.finish()
    biases.finish()


def block_all(sizes, x, tok, cot, wo, w1, w2, vec, rows, qkv, ctx, lse, lengths, weights):
    steps, dp_steps = all_steps(sizes), mesh_steps(sizes, "dp")
    count, dp_count = len(steps), len(dp_steps)
    groups, length, model = rows.shape
    tokens, hidden = x.shape[0], w1.shape[1]
    tiles = hidden // model
    layout = Layout(sizes, hidden, model)
    block, joint_width = length // sizes["head"], 3 * weights[0].shape[0]
    devices = sizes["dp"] * sizes["head"]
    head_rows = round_up(model // sizes["dp"], 16)
    unit = part_rows(head_rows)
    parts = head_rows // unit
    small_rows = 8 + tiles
    dma = pltpu.SemaphoreType.DMA
    shape = jax.ShapeDtypeStruct
    vmem = pltpu.VMEM
    tall = max(tokens, layout.tall)
    return pl.pallas_call(
        functools.partial(block_kernel, sizes, layout),
        out_shape=[
            shape((tokens, model), BF16),
            shape((tokens, model), F32),
            shape((layout.rows, model), F32),
            shape((parts, unit, joint_width), F32),
            shape((small_rows, model), F32),
            shape((8, joint_width), F32),
        ],
        in_specs=[ANY] * 6 + [VMEM] + [ANY] * 3 + [VMEM, SMEM] + [ANY] * 3,
        out_specs=[ANY, ANY] + [VMEM] * 4,
        scratch_shapes=[
            vmem((tiles, tall, model), BF16),
            vmem((tiles, tall, model), BF16),
            vmem((16, 128) if layout.slack else (devices, layout.out_pad, model), BF16),
            vmem((2, 2, model, model), BF16),
            vmem((model, model), BF16),
            vmem((tokens, model), BF16),
            vmem((tokens, model), BF16),
            vmem((tokens, model), BF16),
            vmem((tokens, model), BF16),
            vmem((tokens, model), F32),
            vmem((tokens, model), F32),
            vmem((tokens, 1), F32),
            vmem(tok.shape, BF16),
            vmem((tokens, model), BF16),
            vmem((small_rows, model), F32),
            vmem((length, 128), F32),
            vmem(tok.shape, BF16),
            vmem((model, joint_width), F32),
            vmem((8, joint_width), F32),
            vmem((8, joint_width), F32),
            vmem((joint_width, model), BF16),
            vmem((2, joint_width, length), BF16),
            vmem((2,) + tok.shape[1:], BF16),
            vmem((2, 2 * block, model), BF16),
            vmem((2, block, model), BF16),
            vmem((parts, sizes["dp"], unit, joint_width), BF16),
        ]
        + [vmem((devices >> (k + 1), layout.rows, model), BF16) for k in range(count)]
        + [vmem((parts, sizes["dp"] >> (k + 1), unit, joint_width), BF16) for k in range(dp_count)]
        + [vmem((count, small_rows, model), F32)] * 2
        + [vmem((count, 8, joint_width), F32)] * 2
        + [dma((3, tiles))] * 2
        + [dma((layout.parts, count))] * 2
        + [dma((parts, dp_count))] * 2
        + [dma((count,))] * 4
        + [dma((groups, 3))] * 2
        + [dma((groups,))] * 4
        + [dma((7,)), dma((2, 2)), dma((2, 3)), dma, dma((groups,))],
        compiler_params=pltpu.CompilerParams(
            collective_id=1, has_side_effects=True, vmem_limit_bytes=60 * MIB
        ),
    )(x, tok, cot, wo, w1, w2, vec, rows, qkv, ctx, lse, lengths, *weights)


def last_kernel(
    layout,
    out_in,
    dx_in,
    wide_in,
    head_in,
    small_in,
    bias_in,
    out_ref,
    dx_ref,
    wq_ref,
    wk_ref,
    wv_ref,
    qb_ref,
    vb_ref,
    outer_ref,
    inner_ref,
    wo_ref,
    inner_bias_ref,
    *sums,
):
    out_ref[...] = out_in[...]
    dx_ref[...] = dx_in[...]
    model = out_in.shape[1]

    @pl.when(pl.program_id(0) == 0)
    def _():
        count, width = wq_ref.shape
        for i, ref in enumerate((wq_ref, wk_ref, wv_ref)):
            ref[...] = head_in[:count, i * width : (i + 1) * width]
        for i in range(qb_ref.shape[1] // width):
            at = slice(i * width, (i + 1) * width)
            qb_ref[:, at] = bias_in[i : i + 1, :width]
            vb_ref[:, at] = bias_in[i : i + 1, 2 * width :]
        outer_ref[...] = wide_in[: layout.per]
        inner_ref[...] = wide_in[layout.pad : layout.pad + layout.per]
        wo_ref[...] = wide_in[layout.out_at : layout.out_at + layout.per_out]
        for j in range(small_in.shape[0] - 8):
            inner_bias_ref[:, j * model : (j + 1) * model] = small_in[8 + j : 9 + j]
        for row, ref in zip((0, 1, 2, 4, 5, 6), sums):
            ref[...] = small_in[row : row + 1]


def last_all(sizes, layout, out, dx, wide, head_part, small, biases):
    tokens, model = out.shape
    width = head_part.shape[1] // 3
    hidden = (small.shape[0] - 8) * model
    shape = jax.ShapeDtypeStruct
    shapes = (
        [shape((tokens, model), BF16), shape((tokens, model), F32)]
        + [shape((model // sizes["dp"], width), F32)] * 3
        + [shape((1, model), F32)] * 2
        + [shape((layout.per, model), F32)] * 2
        + [shape((layout.per_out, model), F32), shape((1, hidden), F32)]
        + [shape((1, model), F32)] * 6
    )
    steps = 7 if tokens % (7 * 16) == 0 else 1
    rows = pl.BlockSpec((tokens // steps, model), lambda i: (i, 0))

    def whole(array):
        return pl.BlockSpec(array.shape, lambda i: (0, 0))

    return pl.pallas_call(
        functools.partial(last_kernel, layout),
        grid=(steps,),
        out_shape=shapes,
        in_specs=[rows, rows] + [whole(a) for a in (wide, head_part, small, biases)],
        out_specs=[rows, rows] + [whole(a) for a in shapes[2:]],
        compiler_params=pltpu.CompilerParams(vmem_limit_bytes=30 * MIB),
    )(out, dx, wide, head_part, small, biases)


def store_chunk(wide_ref, place, base, rows, values):
    unit = wide_ref.shape[2]
    at = 0
    while at < rows:
        part, low = divmod(base + at, unit)
        count = min(rows - at, unit - low)
        wide_ref[part, place, low : low + count] = values[at : at + count]
        at += count


def round_up(value, unit):
    return -(-value // unit) * unit


def part_rows(rows):
    return 32 if rows % 32 == 0 else 16


def on_device(
    sizes,
    inputs,
    lengths,
    query_weight,
    query_bias,
    key_weight,
    value_weight,
    value_bias,
    attention_out_weight,
    output_bias,
    first_gain,
    first_shift,
    expand_weight,
    inner_bias,
    contract_weight,
    outer_bias,
    second_gain,
    second_shift,
    cotangent,
):
    groups, block, model = inputs.shape
    hidden = expand_weight.shape[1]
    flat = (groups * block, model)
    weights = [query_weight.T, key_weight.T, value_weight.T]
    pieces = (
        output_bias,
        first_gain,
        first_shift,
        outer_bias,
        second_gain,
        second_shift,
        inner_bias,
        query_bias,
        value_bias,
    )
    total = sum(piece.shape[0] for piece in pieces)
    vec, at = jnp.zeros((total,), F32), 0
    for piece in pieces:
        end = at + piece.shape[0]
        vec = vec + jnp.pad(piece.astype(F32), (at, total - end))
        at = end
    vec = vec[None]
    rows, qkv, ctx, lse, tok = attend_all(sizes, inputs, lengths, weights, vec)
    out, dx, wide, head_part, small, biases = block_all(
        sizes,
        inputs.reshape(flat),
        tok,
        cotangent.reshape(flat),
        attention_out_weight,
        expand_weight,
        contract_weight,
        vec,
        rows,
        qkv,
        ctx,
        lse,
        lengths,
        weights,
    )
    head_part = head_part.reshape(-1, head_part.shape[2])
    layout = Layout(sizes, hidden, model)
    (out, dx, wq, wk, wv, query_sum, value_sum, outer, inner, wo, inner_sum, *sums) = last_all(
        sizes, layout, out, dx, wide, head_part, small, biases
    )
    sums = [s.reshape(-1) for s in sums]
    return (
        out.reshape(inputs.shape),
        dx.reshape(inputs.shape),
        wq,
        query_sum.reshape(-1),
        wk,
        wv,
        value_sum.reshape(-1),
        wo.T,
        sums[0],
        sums[1],
        sums[2],
        inner.T,
        inner_sum.reshape(-1),
        outer,
        sums[3],
        sums[4],
        sums[5],
    )


def solution(mesh):
    in_specs = (
        P("dp", "head", None),
        P("dp"),
        P(None, "head"),
        P("head"),
        P(None, "head"),
        P(None, "head"),
        P("head"),
        P(),
        P(),
        P(),
        P(),
        P(),
        P(),
        P(),
        P(),
        P(),
        P(),
        P("dp", "head", None),
    )
    out_specs = (
        P("dp", "head", None),
        P("dp", "head", None),
        P("dp", "head"),
        P(),
        P("dp", "head"),
        P("dp", "head"),
        P(),
        P(None, ("dp", "head")),
        P(),
        P(),
        P(),
        P(None, ("dp", "head")),
        P(),
        P(("dp", "head"), None),
        P(),
        P(),
        P(),
    )
    return jax.shard_map(
        functools.partial(on_device, dict(mesh.shape)), mesh=mesh, in_specs=in_specs, out_specs=out_specs, check_vma=False
    )
```

time: 260 us -> 231 us (0.89)
  Pallas kernels: 234 us -> 217 us
  local copies, waits for them, and re-layouts: 21.1 us -> 7.31 us
    pallas_call x2, Pallas kernels: 181 us -> 165 us  [the longest x1 161 us: block_all(): pl.pallas_call(functools.partial(block_kernel, sizes, layout), out_shape=...]
    slice x5 -> x0, local copies, waits for them, and re-layouts: 6.87 us -> none  [the longest x1 1.9 us: on_device(): wide[:inner]]
    pallas_call x0 -> x8, other arithmetic: none -> 4.84 us  [last_all(): pl.pallas_call(functools.partial(last_kernel, layout), grid=(steps,), out...]
    another operation x8 -> x0, local copies, waits for them, and re-layouts: 4.27 us -> none  [on_device(): jnp.stack([output_bias, first_gain, first_shift, outer_bias, second_gain,...]
    unnamed x13 -> x12, local copies, waits for them, and re-layouts: 6.38 us -> 6.68 us
where the time goes in v3:
time: 231 us; the launch traced here: 230 us
  Pallas kernels  217 us (94%)
  local copies, waits for them, and re-layouts  7.31 us (3%)
  other arithmetic  5.73 us (2%)
    pallas_call x1, Pallas kernels, block_all(): pl.pallas_call(functools.partial(block_kernel, sizes, layout), out_shape=...  161 us
    pallas_call x1, Pallas kernels, attend_all(): pl.pallas_call(functools.partial(attend_kernel, steps), out_shape=[shape(...  51.5 us
    unnamed x12, local copies, waits for them, and re-layouts  6.68 us
    pallas_call x8, other arithmetic, last_all(): pl.pallas_call(functools.partial(last_kernel, layout), grid=(steps,), out...  4.84 us

profile of v3, /device:TPU:0, one launch (start us, length us, event | category | flops | bytes accessed | tf_op | source)
XLA Modules:
  0.0 230.3 jit_solution(690419532218171788)
XLA Ops:
  0.7 0.9 convert_add_fusion
  1.6 0.6 broadcast_in_dim.3.vec_ref
  2.2 51.5 %shard_map.305 = (bf16[7,512,768]{2,1,0:T(8,128)(2,1)}, bf16[7,576,512]{2,1,0:T(8,128)(2,1)}, bf16[7,4,192,128]{3,2,1,0:T(8,128)(2,1)}, f32[7,3,512]{2,1,0:T(4,128)}, bf16[7,4,192,128]{3,2,1,0:T(8,128)(2,1)}) custom-call(bf16[7,128,768]{2,1,0:T(8,128)(2,1)} %x_ref.1, s32[7]{0:T(128)} %len_ref.3, bf16[192,768]{1,0:T(8,128)(2,1)} %bitcast.14, ...), custom_call_target="tpu_custom_call" | custom-call | tf_op jit(solution)/shard_map/pallas_call | solution.py:470
  53.7 161.3 %shard_map.306 = (bf16[896,768]{1,0:T(8,128)(2,1)}, f32[896,768]{1,0:T(8,128)}, f32[224,768]{1,0:T(8,128)}, f32[3,32,576]{2,1,0:T(8,128)}, f32[12,768]{1,0:T(8,128)}, /*index=5*/f32[8,576]{1,0:T(8,128)}) custom-call(bf16[896,768]{1,0:T(8,128)(2,1)} %bitcast.12, bf16[7,4,192,128]{3,2,1,0:T(8,128)(2,1)} %get-tuple-element.45.tok_ref, ...), custom_call_target="tpu_custom_call" | custom-call | tf_op jit(solution)/shard_map/pallas_call | solution.py:975
  215.0 0.0 copy-start
  215.0 1.8 copy-done
  216.8 0.0 copy-start.1
  216.8 1.3 copy-done.1
  218.1 0.0 copy-start.2
  218.1 1.1 copy-done.2
  219.2 0.0 copy-start.3
  219.2 0.9 copy-done.3
  220.2 0.0 copy-start.4
  220.2 0.8 copy-done.4
  221.0 0.0 copy-start.5
  221.0 0.7 copy-done.5
  221.7 3.8 %shard_map.307 = (bf16[896,768]{1,0:T(8,128)(2,1)}, f32[896,768]{1,0:T(8,128)}, f32[96,192]{1,0:T(8,128)}, f32[96,192]{1,0:T(8,128)}, f32[96,192]{1,0:T(8,128)},...) custom-call(bf16[896,768]{1,0:T(8,128)(2,1)S(1)} %copy-done.1, ...), custom_call_target="tpu_custom_call" | custom-call | tf_op jit(solution)/shard_map/pallas_call | solution.py:1094
  225.5 0.6 reduce
  226.1 0.6 reduce.1
  226.7 0.6 reduce.2
  227.3 0.6 reduce.3
  227.9 0.6 reduce.4
  228.5 0.6 reduce.5
  229.1 0.6 reduce.6
  229.7 0.6 reduce.7
Async XLA Ops:
  215.0 1.8 copy-start
  216.8 1.3 copy-start.1
  218.1 1.1 copy-start.2
  219.2 0.9 copy-start.3
  220.2 0.8 copy-start.4
  221.0 0.7 copy-start.5

commit v4 on v3

--- a/solution.py
+++ b/solution.py
@@ -522,7 +522,6 @@
     wide_out,
     head_out,
     small_out,
-    bias_out,
     active,
     slope,
     out_grad,
@@ -542,7 +541,6 @@
     dctx,
     weight_sum,
     bias_sum,
-    bias_full,
     w_ref,
     qkv_slots,
     ctx_slots,
@@ -555,8 +553,8 @@
     count = len(steps)
     wide_land, scratch = scratch[:count], scratch[count:]
     head_land, scratch = scratch[: len(dp_steps)], scratch[len(dp_steps) :]
-    small_land, small_total, bias_land, bias_total = scratch[:4]
-    sems = scratch[4:]
+    small_land, small_total = scratch[:2]
+    sems = scratch[2:]
     groups, length, model = rows_ref.shape
     hidden = w1_ref.shape[1]
     width = wq_ref.shape[0]
@@ -570,10 +568,11 @@
     low_bit, high_bit = bit_of(head_steps[0]), bit_of(head_steps[1])
     wide = Wide(sizes, layout, steps, [active, slope, out_grad], wide_land, sems[:4], wide_out)
     head = Scatter(dp_steps, head_src, head_land, sems[4], sems[5], head_out)
-    small = Everywhere(steps, small_in, small_land, small_total, sems[6], sems[7], small_out)
-    biases = Everywhere(steps, bias_full, bias_land, bias_total, sems[8], sems[9], bias_out)
-    tok_send, tok_recv, near_send, near_recv, far_send, far_recv = sems[10:16]
-    load_sem, slot_sem, seq_sem, out_sem, dx_sem = sems[16:]
+    small = Everywhere(
+        dp_steps + head_steps, small_in, small_land, small_total, sems[6], sems[7], small_out
+    )
+    tok_send, tok_recv, near_send, near_recv, far_send, far_recv = sems[8:14]
+    load_sem, slot_sem, seq_sem, out_sem, dx_sem = sems[14:]
     dx_part = normed
 
     output_bias, gain1, shift1, outer_bias, gain2, shift2 = [
@@ -783,7 +782,6 @@
         return carry
 
     lax.fori_loop(0, 2, third, 0)
-    small.copy(0).start()
 
     def context_back(h, carry):
         rows = pl.ds(pl.multiple_of(h * width, 16), width)
@@ -886,24 +884,14 @@
         far_copy(s).start()
         rows = block_rows(s)
         branch[rows] = branch[rows] + dx_part[mine] + landed_mine.astype(F32)
-        for level in range(count):
-
-            @pl.when(s == level)
-            def _():
-                small.land(level)
-                if level + 1 < count:
-                    small.copy(level + 1).start()
-
         return carry
 
     def dx_copy(s):
         return pltpu.make_async_copy(branch.at[block_rows(s)], dx_ref.at[block_rows(s)], dx_sem.at[s])
 
     lax.fori_loop(0, groups, sequence, 0)
-    for level in range(groups, count):
-        small.land(level)
-        if level + 1 < count:
-            small.copy(level + 1).start()
+    small_in[pl.ds(8 + tiles + me, 1), : 3 * width] = bias_sum[0:1]
+    small.copy(0).start()
     unit = head_src.shape[2]
     rows = model // sizes["dp"]
     for dp in range(sizes["dp"]):
@@ -917,9 +905,6 @@
             )
     for part in range(head.parts):
         head.start(part, 0)
-    bias_full[...] = jnp.zeros_like(bias_full)
-    bias_full[pl.ds(me, 1)] = bias_sum[0:1]
-    biases.copy(0).start()
     last = groups - 1
     far_copy(last).wait_recv()
     branch[last * block :] = branch[last * block :] + far_land[last % 2].astype(F32)
@@ -934,9 +919,9 @@
                 if level + 1 < len(dp_steps):
                     head.start(part, level + 1)
         if t < count:
-            biases.land(t)
+            small.land(t)
             if t + 1 < count:
-                biases.copy(t + 1).start()
+                small.copy(t + 1).start()
 
     def finish(s, carry):
         dx_copy(s).wait()
@@ -952,7 +937,6 @@
     wide.finish(tiles)
     head.finish()
     small.finish()
-    biases.finish()
 
 
 def block_all(sizes, x, tok, cot, wo, w1, w2, vec, rows, qkv, ctx, lse, lengths, weights):
@@ -967,7 +951,7 @@
     head_rows = round_up(model // sizes["dp"], 16)
     unit = part_rows(head_rows)
     parts = head_rows // unit
-    small_rows = 8 + tiles
+    small_rows = 8 + tiles + sizes["head"]
     dma = pltpu.SemaphoreType.DMA
     shape = jax.ShapeDtypeStruct
     vmem = pltpu.VMEM
@@ -980,10 +964,9 @@
             shape((layout.rows, model), F32),
             shape((parts, unit, joint_width), F32),
             shape((small_rows, model), F32),
-            shape((8, joint_width), F32),
         ],
         in_specs=[ANY] * 6 + [VMEM] + [ANY] * 3 + [VMEM, SMEM] + [ANY] * 3,
-        out_specs=[ANY, ANY] + [VMEM] * 4,
+        out_specs=[ANY, ANY] + [VMEM] * 3,
         scratch_shapes=[
             vmem((tiles, tall, model), BF16),
             vmem((tiles, tall, model), BF16),
@@ -1004,7 +987,6 @@
             vmem(tok.shape, BF16),
             vmem((model, joint_width), F32),
             vmem((8, joint_width), F32),
-            vmem((8, joint_width), F32),
             vmem((joint_width, model), BF16),
             vmem((2, joint_width, length), BF16),
             vmem((2,) + tok.shape[1:], BF16),
@@ -1015,11 +997,10 @@
         + [vmem((devices >> (k + 1), layout.rows, model), BF16) for k in range(count)]
         + [vmem((parts, sizes["dp"] >> (k + 1), unit, joint_width), BF16) for k in range(dp_count)]
         + [vmem((count, small_rows, model), F32)] * 2
-        + [vmem((count, 8, joint_width), F32)] * 2
         + [dma((3, tiles))] * 2
         + [dma((layout.parts, count))] * 2
         + [dma((parts, dp_count))] * 2
-        + [dma((count,))] * 4
+        + [dma((count,))] * 2
         + [dma((groups, 3))] * 2
         + [dma((groups,))] * 4
         + [dma((7,)), dma((2, 2)), dma((2, 3)), dma, dma((groups,))],
@@ -1036,7 +1017,6 @@
     wide_in,
     head_in,
     small_in,
-    bias_in,
     out_ref,
     dx_ref,
     wq_ref,
@@ -1059,46 +1039,46 @@
         count, width = wq_ref.shape
         for i, ref in enumerate((wq_ref, wk_ref, wv_ref)):
             ref[...] = head_in[:count, i * width : (i + 1) * width]
-        for i in range(qb_ref.shape[1] // width):
+        for i in range(qb_ref.shape[0] // width):
             at = slice(i * width, (i + 1) * width)
-            qb_ref[:, at] = bias_in[i : i + 1, :width]
-            vb_ref[:, at] = bias_in[i : i + 1, 2 * width :]
+            row = small_in.shape[0] - qb_ref.shape[0] // width + i
+            qb_ref[at] = small_in[row, :width]
+            vb_ref[at] = small_in[row, 2 * width : 3 * width]
         outer_ref[...] = wide_in[: layout.per]
         inner_ref[...] = wide_in[layout.pad : layout.pad + layout.per]
         wo_ref[...] = wide_in[layout.out_at : layout.out_at + layout.per_out]
-        for j in range(small_in.shape[0] - 8):
-            inner_bias_ref[:, j * model : (j + 1) * model] = small_in[8 + j : 9 + j]
+        for j in range(inner_bias_ref.shape[0] // model):
+            inner_bias_ref[j * model : (j + 1) * model] = small_in[8 + j]
         for row, ref in zip((0, 1, 2, 4, 5, 6), sums):
-            ref[...] = small_in[row : row + 1]
-
-
-def last_all(sizes, layout, out, dx, wide, head_part, small, biases):
+            ref[...] = small_in[row]
+
+
+def last_all(sizes, layout, hidden, out, dx, wide, head_part, small):
     tokens, model = out.shape
     width = head_part.shape[1] // 3
-    hidden = (small.shape[0] - 8) * model
     shape = jax.ShapeDtypeStruct
     shapes = (
         [shape((tokens, model), BF16), shape((tokens, model), F32)]
         + [shape((model // sizes["dp"], width), F32)] * 3
-        + [shape((1, model), F32)] * 2
+        + [shape((model,), F32)] * 2
         + [shape((layout.per, model), F32)] * 2
-        + [shape((layout.per_out, model), F32), shape((1, hidden), F32)]
-        + [shape((1, model), F32)] * 6
+        + [shape((layout.per_out, model), F32), shape((hidden,), F32)]
+        + [shape((model,), F32)] * 6
     )
     steps = 7 if tokens % (7 * 16) == 0 else 1
     rows = pl.BlockSpec((tokens // steps, model), lambda i: (i, 0))
 
     def whole(array):
-        return pl.BlockSpec(array.shape, lambda i: (0, 0))
+        return pl.BlockSpec(array.shape, lambda i: (0,) * len(array.shape))
 
     return pl.pallas_call(
         functools.partial(last_kernel, layout),
         grid=(steps,),
         out_shape=shapes,
-        in_specs=[rows, rows] + [whole(a) for a in (wide, head_part, small, biases)],
+        in_specs=[rows, rows] + [whole(a) for a in (wide, head_part, small)],
         out_specs=[rows, rows] + [whole(a) for a in shapes[2:]],
-        compiler_params=pltpu.CompilerParams(vmem_limit_bytes=30 * MIB),
-    )(out, dx, wide, head_part, small, biases)
+        compiler_params=pltpu.CompilerParams(vmem_limit_bytes=60 * MIB),
+    )(out, dx, wide, head_part, small)
 
 
 def store_chunk(wide_ref, place, base, rows, values):
@@ -1163,7 +1143,7 @@
         at = end
     vec = vec[None]
     rows, qkv, ctx, lse, tok = attend_all(sizes, inputs, lengths, weights, vec)
-    out, dx, wide, head_part, small, biases = block_all(
+    out, dx, wide, head_part, small = block_all(
         sizes,
         inputs.reshape(flat),
         tok,
@@ -1182,23 +1162,22 @@
     head_part = head_part.reshape(-1, head_part.shape[2])
     layout = Layout(sizes, hidden, model)
     (out, dx, wq, wk, wv, query_sum, value_sum, outer, inner, wo, inner_sum, *sums) = last_all(
-        sizes, layout, out, dx, wide, head_part, small, biases
+        sizes, layout, hidden, out, dx, wide, head_part, small
     )
-    sums = [s.reshape(-1) for s in sums]
     return (
         out.reshape(inputs.shape),
         dx.reshape(inputs.shape),
         wq,
-        query_sum.reshape(-1),
+        query_sum,
         wk,
         wv,
-        value_sum.reshape(-1),
+        value_sum,
         wo.T,
         sums[0],
         sums[1],
         sums[2],
         inner.T,
-        inner_sum.reshape(-1),
+        inner_sum,
         outer,
         sums[3],
         sums[4],

time: 231 us -> 196 us (0.85)
  Pallas kernels: 217 us -> 193 us
  local copies, waits for them, and re-layouts: 7.31 us -> 0.63 us
  other arithmetic: 5.73 us -> 0.89 us
    pallas_call x1, Pallas kernels: 161 us -> 135 us  [block_all(): pl.pallas_call(functools.partial(block_kernel, sizes, layout), out_shape=...]
    unnamed x12 -> x0, local copies, waits for them, and re-layouts: 6.68 us -> none
    pallas_call x8 -> x0, other arithmetic: 4.84 us -> none  [last_all(): pl.pallas_call(functools.partial(last_kernel, layout), grid=(steps,), out...]
    pallas_call x1, Pallas kernels: 3.81 us -> 7.13 us  [last_all(): pl.pallas_call(functools.partial(last_kernel, layout), grid=(steps,), out...]
where the time goes in v4:
time: 196 us
  Pallas kernels  193 us (98%)
    pallas_call x1, Pallas kernels, block_all(): pl.pallas_call(functools.partial(block_kernel, sizes, layout), out_shape=...  135 us
    pallas_call x1, Pallas kernels, attend_all(): pl.pallas_call(functools.partial(attend_kernel, steps), out_shape=[shape(...  51.5 us
    pallas_call x1, Pallas kernels, last_all(): pl.pallas_call(functools.partial(last_kernel, layout), grid=(steps,), out...  7.13 us

profile of v4, /device:TPU:0, one launch (start us, length us, event | category | flops | bytes accessed | tf_op | source)
XLA Modules:
  0.0 195.8 jit_solution(8323691188301787490)
XLA Ops:
  0.7 0.9 convert_add_fusion
  1.6 0.6 broadcast_in_dim.3.vec_ref
  2.2 51.5 %shard_map.305 = (bf16[7,512,768]{2,1,0:T(8,128)(2,1)}, bf16[7,576,512]{2,1,0:T(8,128)(2,1)}, bf16[7,4,192,128]{3,2,1,0:T(8,128)(2,1)}, f32[7,3,512]{2,1,0:T(4,128)}, bf16[7,4,192,128]{3,2,1,0:T(8,128)(2,1)}) custom-call(bf16[7,128,768]{2,1,0:T(8,128)(2,1)} %x_ref.1, s32[7]{0:T(128)} %len_ref.3, bf16[192,768]{1,0:T(8,128)(2,1)} %bitcast.12, ...), custom_call_target="tpu_custom_call" | custom-call | tf_op jit(solution)/shard_map/pallas_call | solution.py:470
  53.7 134.7 %shard_map.306 = (bf16[896,768]{1,0:T(8,128)(2,1)}, f32[896,768]{1,0:T(8,128)}, f32[224,768]{1,0:T(8,128)}, f32[3,32,576]{2,1,0:T(8,128)}, f32[16,768]{1,0:T(8,128)}) custom-call(bf16[896,768]{1,0:T(8,128)(2,1)} %bitcast.10, bf16[7,4,192,128]{3,2,1,0:T(8,128)(2,1)} %get-tuple-element.44.tok_ref, bf16[896,768]{1,0:T(8,128)(2,1)} %bitcast.11, ...), custom_call_target="tpu_custom_call" | custom-call | tf_op jit(solution)/shard_map/pallas_call | solution.py:959
  188.5 7.1 %shard_map.307 = (bf16[896,768]{1,0:T(8,128)(2,1)}, f32[896,768]{1,0:T(8,128)}, f32[96,192]{1,0:T(8,128)}, f32[96,192]{1,0:T(8,128)}, f32[96,192]{1,0:T(8,128)},...) custom-call(bf16[896,768]{1,0:T(8,128)(2,1)} %get-tuple-element.49.o, ...), custom_call_target="tpu_custom_call" | custom-call | tf_op jit(solution)/shard_map/pallas_call | solution.py:1074

commit v5 on v4

--- a/solution.py
+++ b/solution.py
@@ -296,7 +296,7 @@
 
     def turn(self, t):
         for level in reversed(range(1, len(self.steps))):
-            part = t - (level - 1)
+            part = t - 2 * (level - 1)
             if isinstance(t, int):
                 if 0 <= part < self.layout.parts:
                     self.land(part, level)
@@ -537,7 +537,6 @@
     tok,
     cot,
     small_in,
-    mask,
     dctx,
     weight_sum,
     bias_sum,
@@ -677,6 +676,8 @@
         return carry
 
     lax.fori_loop(0, 2, project, 0)
+    spans = [pl.ds(i * (half // 2), half // 2) for i in range(4)]
+    branch[...] = jnp.zeros_like(branch)
 
     def forward(j, carry):
         slot = j % 2
@@ -687,23 +688,26 @@
             start(slot_load(j + 1, 1 - slot))
 
         bias = vec_ref[:, pl.ds(pl.multiple_of((6 + j) * model, model), model)]
-        for i in range(2):
-            rows = pl.ds(i * half, half)
-            h = dot(low_ref[rows], slots[slot, 0], NN) + bias
+        def inward(i):
+            return dot(low_ref[spans[i]], slots[slot, 0], NN) + bias
+
+        def outward(i, a):
+            made = dot(a, slots[slot, 1], NN)
+            branch[spans[i]] = jnp.where(j == 0, 0.0, branch[spans[i]]) + made
+
+        ahead, held = inward(0), None
+        for i, rows in enumerate(spans):
+            h = ahead
+            if i + 1 < len(spans):
+                ahead = inward(i + 1)
             phi = 0.5 + 0.5 * lax.erf(h * 0.7071067811865476)
             a = (h * phi).astype(BF16)
             active[j, rows] = a
             slope[j, rows] = (phi + h * jnp.exp(-0.5 * h * h) * 0.3989422804014327).astype(BF16)
-            made = dot(a, slots[slot, 1], NN)
-
-            @pl.when(j == 0)
-            def _():
-                branch[rows] = made
-
-            @pl.when(j > 0)
-            def _():
-                branch[rows] = branch[rows] + made
-
+            if i:
+                outward(i - 1, held)
+            held = a
+        outward(len(spans) - 1, held)
         return carry
 
     lax.fori_loop(0, tiles, forward, 0)
@@ -824,8 +828,13 @@
         def _():
             start(sequence_load(s + 1))
 
-        fill_mask(len_ref[s], mask)
-        for h in range(heads):
+        first_row = lax.broadcasted_iota(jnp.int32, (16, length), 0) == 0
+        hidden_key = lax.broadcasted_iota(jnp.int32, (16, length), 1) >= len_ref[s]
+        mask_rows = jnp.where(first_row & hidden_key, MASKED, 0.0).astype(BF16)
+        one_rows = jnp.where(first_row, 1.0, 0.0).astype(BF16)
+        span = length // 2
+
+        def load(h):
             at = h * HEAD_DIM
             q = qkv_slots[slot, at : at + HEAD_DIM]
             k = qkv_slots[slot, width + at : width + at + HEAD_DIM]
@@ -834,15 +843,42 @@
             d_ctx = jnp.concatenate([dctx[s, d, part] for d in range(length // block)], axis=1)
             ctx = jnp.concatenate([ctx_slots[slot, d, part] for d in range(length // block)], axis=1)
             delta = jnp.sum(d_ctx.astype(F32) * ctx.astype(F32), axis=0, keepdims=True)
-            scores = dot(k.T, q, NN) + widen(mask[...], length)
-            weights = jnp.exp(scores - lse_ref[s, h : h + 1])
-            d_weights = dot(v.T, d_ctx, NN)
-            d_scores = (weights * (d_weights - delta)).astype(BF16)
-            qkv_slots[slot, at : at + HEAD_DIM] = (dot(k, d_scores, NN) * SCALE).astype(BF16)
-            qkv_slots[slot, width + at : width + at + HEAD_DIM] = dot(q, d_scores, NT).astype(BF16)
-            qkv_slots[slot, 2 * width + at : 2 * width + at + HEAD_DIM] = dot(
-                d_ctx, weights.astype(BF16), NT
-            ).astype(BF16)
+            k_masked = jnp.concatenate([k, mask_rows], axis=0).T
+            q_masked = jnp.concatenate([q, one_rows], axis=0)
+            return q, k, d_ctx, delta, k_masked, q_masked, v.T
+
+        def products(head, i):
+            _, _, d_ctx, _, k_masked, q_masked, v_turned = head
+            keys = slice(i * span, (i + 1) * span)
+            return dot(k_masked[keys], q_masked, NN), dot(v_turned[keys], d_ctx, NN)
+
+        now = load(0)
+        ahead = products(now, 0)
+        d_query = None
+        for h in range(heads):
+            at = h * HEAD_DIM
+            q, k, d_ctx, delta = now[:4]
+            following = None
+            for i in range(2):
+                scores, d_weights = ahead
+                if i == 0:
+                    ahead = products(now, 1)
+                elif h + 1 < heads:
+                    following = load(h + 1)
+                    ahead = products(following, 0)
+                keys = slice(i * span, (i + 1) * span)
+                weights = jnp.exp(scores - lse_ref[s, h : h + 1])
+                d_scores = (weights * (d_weights - delta)).astype(BF16)
+                qkv_slots[slot, width + at : width + at + HEAD_DIM, keys] = dot(
+                    q, d_scores, NT
+                ).astype(BF16)
+                qkv_slots[slot, 2 * width + at : 2 * width + at + HEAD_DIM, keys] = dot(
+                    d_ctx, weights.astype(BF16), NT
+                ).astype(BF16)
+                piece = dot(k[:, keys], d_scores, NN)
+                d_query = piece if i == 0 else d_query + piece
+            qkv_slots[slot, at : at + HEAD_DIM] = (d_query * SCALE).astype(BF16)
+            now = following
         dx_part[:length] = dot(qkv_slots[slot], w_ref[...], TN)
 
         @pl.when(s >= 2)
@@ -909,7 +945,7 @@
     far_copy(last).wait_recv()
     branch[last * block :] = branch[last * block :] + far_land[last % 2].astype(F32)
     dx_copy(last).start()
-    last_turn = layout.parts + count - 2
+    last_turn = layout.parts + 2 * (count - 2)
     for t in range(max(last_turn - groups, head.parts + len(dp_steps) - 1, count)):
         wide.turn(t + groups)
         for level in reversed(range(len(dp_steps))):
@@ -983,7 +1019,6 @@
             vmem(tok.shape, BF16),
             vmem((tokens, model), BF16),
             vmem((small_rows, model), F32),
-            vmem((length, 128), F32),
             vmem(tok.shape, BF16),
             vmem((model, joint_width), F32),
             vmem((8, joint_width), F32),
@@ -1065,7 +1100,7 @@
         + [shape((layout.per_out, model), F32), shape((hidden,), F32)]
         + [shape((model,), F32)] * 6
     )
-    steps = 7 if tokens % (7 * 16) == 0 else 1
+    steps = 2 if tokens % 32 == 0 else 1
     rows = pl.BlockSpec((tokens // steps, model), lambda i: (i, 0))
 
     def whole(array):

time: 196 us -> 185 us (0.944)
  Pallas kernels: 193 us -> 182 us
    pallas_call x1, Pallas kernels: 135 us -> 126 us  [block_all(): pl.pallas_call(functools.partial(block_kernel, sizes, layout), out_shape=...]
    pallas_call x1, Pallas kernels: 7.13 us -> 4.44 us  [last_all(): pl.pallas_call(functools.partial(last_kernel, layout), grid=(steps,), out...]
where the time goes in v5:
time: 185 us; the launch traced here: 184 us
  Pallas kernels  182 us (98%)
    pallas_call x1, Pallas kernels, block_all(): pl.pallas_call(functools.partial(block_kernel, sizes, layout), out_shape=...  126 us
    pallas_call x1, Pallas kernels, attend_all(): pl.pallas_call(functools.partial(attend_kernel, steps), out_shape=[shape(...  51.5 us
    pallas_call x1, Pallas kernels, last_all(): pl.pallas_call(functools.partial(last_kernel, layout), grid=(steps,), out...  4.44 us

profile of v5, /device:TPU:0, one launch (start us, length us, event | category | flops | bytes accessed | tf_op | source)
XLA Modules:
  0.0 184.5 jit_solution(2560763521339369327)
XLA Ops:
  0.7 0.9 convert_add_fusion
  1.6 0.6 broadcast_in_dim.3.vec_ref
  2.2 51.5 %shard_map.305 = (bf16[7,512,768]{2,1,0:T(8,128)(2,1)}, bf16[7,576,512]{2,1,0:T(8,128)(2,1)}, bf16[7,4,192,128]{3,2,1,0:T(8,128)(2,1)}, f32[7,3,512]{2,1,0:T(4,128)}, bf16[7,4,192,128]{3,2,1,0:T(8,128)(2,1)}) custom-call(bf16[7,128,768]{2,1,0:T(8,128)(2,1)} %x_ref.1, s32[7]{0:T(128)} %len_ref.3, bf16[192,768]{1,0:T(8,128)(2,1)} %bitcast.12, ...), custom_call_target="tpu_custom_call" | custom-call | tf_op jit(solution)/shard_map/pallas_call | solution.py:470
  53.7 126.1 %shard_map.306 = (bf16[896,768]{1,0:T(8,128)(2,1)}, f32[896,768]{1,0:T(8,128)}, f32[224,768]{1,0:T(8,128)}, f32[3,32,576]{2,1,0:T(8,128)}, f32[16,768]{1,0:T(8,128)}) custom-call(bf16[896,768]{1,0:T(8,128)(2,1)} %bitcast.10, bf16[7,4,192,128]{3,2,1,0:T(8,128)(2,1)} %get-tuple-element.44.tok_ref, bf16[896,768]{1,0:T(8,128)(2,1)} %bitcast.11, ...), custom_call_target="tpu_custom_call" | custom-call | tf_op jit(solution)/shard_map/pallas_call | solution.py:995
  179.8 4.4 %shard_map.307 = (bf16[896,768]{1,0:T(8,128)(2,1)}, f32[896,768]{1,0:T(8,128)}, f32[96,192]{1,0:T(8,128)}, f32[96,192]{1,0:T(8,128)}, f32[96,192]{1,0:T(8,128)},...) custom-call(bf16[896,768]{1,0:T(8,128)(2,1)} %get-tuple-element.49.o, ...), custom_call_target="tpu_custom_call" | custom-call | tf_op jit(solution)/shard_map/pallas_call | solution.py:1109

commit v6 on v5

--- a/solution.py
+++ b/solution.py
@@ -162,6 +162,17 @@
 
 def widen(tile, width):
     return jnp.concatenate([tile] * (width // tile.shape[1]), axis=1)
+
+
+def each_of(count, step):
+    few = 4 if count % 4 == 0 else count
+
+    def several(i, carry):
+        for j in range(few):
+            step(i * few + j)
+        return carry
+
+    lax.fori_loop(0, count // few, several, 0)
 
 
 class Layout:
@@ -253,13 +264,11 @@
         for low in range(0, rows, unit):
             at = pl.ds(base + low, unit)
 
-            def add(place, carry, low=low, at=at):
+            def add(place, low=low, at=at):
                 mine = self.own(array, self.pair(place), bit, low, unit)[...]
-                total = self.landing[0][place, at].astype(F32) + mine.astype(F32)
-                self.landing[0][place, at] = total.astype(BF16)
-                return carry
-
-            lax.fori_loop(0, self.landing[0].shape[0], add, 0)
+                self.landing[0][place, at] = self.landing[0][place, at] + mine
+
+            each_of(self.landing[0].shape[0], add)
             self.copy((base + low) // unit, 1).start()
 
     def copy(self, part, level):
@@ -282,15 +291,13 @@
         rows = self.rows_of(part)
         last = level == len(self.steps) - 1
 
-        def add(i, carry):
-            total = landed[i, rows].astype(F32) + block[mine + i, rows].astype(F32)
+        def add(i):
             if last:
-                self.result[rows] = total
+                self.result[rows] = landed[i, rows].astype(F32) + block[mine + i, rows].astype(F32)
             else:
-                landed[i, rows] = total.astype(BF16)
-            return carry
-
-        lax.fori_loop(0, count // 2, add, 0)
+                landed[i, rows] = landed[i, rows] + block[mine + i, rows]
+
+        each_of(count // 2, add)
         if not last:
             self.copy(part, level + 1).start()
 
@@ -319,7 +326,7 @@
 
 
 def vector(vec_ref, model, index):
-    return vec_ref[:, index * model : (index + 1) * model]
+    return vec_ref[index * model : (index + 1) * model].reshape(1, model)
 
 
 def attend_kernel(
@@ -398,10 +405,10 @@
     w_ref[:width] = wq_ref[...]
     w_ref[width : 2 * width] = wk_ref[...]
     w_ref[2 * width :] = wv_ref[...]
-    at = vec_ref.shape[1] - 2 * width
-    b_ref[:width] = jnp.broadcast_to(vec_ref[:, at : at + width], (128, width)).T
+    at = vec_ref.shape[0] - 2 * width
+    b_ref[:width] = jnp.broadcast_to(vec_ref[at : at + width].reshape(1, width), (128, width)).T
     b_ref[width : 2 * width] = jnp.zeros((width, 128), F32)
-    b_ref[2 * width :] = jnp.broadcast_to(vec_ref[:, at + width :], (128, width)).T
+    b_ref[2 * width :] = jnp.broadcast_to(vec_ref[at + width :].reshape(1, width), (128, width)).T
     far_copy(0).wait_recv()
     relay_copy(0).start()
 
@@ -687,7 +694,7 @@
         def _():
             start(slot_load(j + 1, 1 - slot))
 
-        bias = vec_ref[:, pl.ds(pl.multiple_of((6 + j) * model, model), model)]
+        bias = vec_ref[pl.ds(pl.multiple_of((6 + j) * model, model), model)].reshape(1, model)
         def inward(i):
             return dot(low_ref[spans[i]], slots[slot, 0], NN) + bias
 
@@ -787,14 +794,15 @@
 
     lax.fori_loop(0, 2, third, 0)
 
-    def context_back(h, carry):
-        rows = pl.ds(pl.multiple_of(h * width, 16), width)
+    def context_back(i, carry):
+        rows = pl.ds(pl.multiple_of(2 * i * width, 16), 2 * width)
         made = dot(wo[rows], attended[...], NT).astype(BF16)
-        for s in range(groups):
-            tok[s, h] = made[:, s * block : (s + 1) * block]
+        for h in range(2):
+            for s in range(groups):
+                tok[s, 2 * i + h] = made[h * width : (h + 1) * width, s * block : (s + 1) * block]
         return carry
 
-    lax.fori_loop(0, sizes["head"], context_back, 0)
+    lax.fori_loop(0, sizes["head"] // 2, context_back, 0)
 
     def begin(s, carry):
         for way in range(3):
@@ -889,7 +897,7 @@
             theirs = pl.ds(pl.multiple_of((2 * i + 1 - low_bit) * block, block), block)
             slots[slot, 1, i * block : (i + 1) * block] = dx_part[theirs].astype(BF16)
         near_copy(s).start()
-        weight_sum[...] += dot(slots[slot, 0, :length], qkv_slots[slot], ((0,), (1,)))
+        weight_sum[...] += dot(qkv_slots[slot], slots[slot, 0, :length], NN)
         bias_sum[...] += dot(jnp.ones((8, length), BF16), qkv_slots[slot], NT)
 
         @pl.when(s == 0)
@@ -930,11 +938,12 @@
     small.copy(0).start()
     unit = head_src.shape[2]
     rows = model // sizes["dp"]
+    turned = weight_sum[...].T.astype(BF16)
     for dp in range(sizes["dp"]):
         place = 0
         for k in range(len(dp_steps)):
             place = place * 2 + (dp >> k) % 2
-        store_chunk(head_src, place, 0, rows, weight_sum[dp * rows : (dp + 1) * rows].astype(BF16))
+        store_chunk(head_src, place, 0, rows, turned[dp * rows : (dp + 1) * rows])
         if rows % unit:
             head_src[head_src.shape[0] - 1, place, rows % unit :] = jnp.zeros(
                 (unit - rows % unit, 3 * width), BF16
@@ -1020,7 +1029,7 @@
             vmem((tokens, model), BF16),
             vmem((small_rows, model), F32),
             vmem(tok.shape, BF16),
-            vmem((model, joint_width), F32),
+            vmem((joint_width, model), F32),
             vmem((8, joint_width), F32),
             vmem((joint_width, model), BF16),
             vmem((2, joint_width, length), BF16),
@@ -1176,7 +1185,6 @@
         end = at + piece.shape[0]
         vec = vec + jnp.pad(piece.astype(F32), (at, total - end))
         at = end
-    vec = vec[None]
     rows, qkv, ctx, lse, tok = attend_all(sizes, inputs, lengths, weights, vec)
     out, dx, wide, head_part, small = block_all(
         sizes,

time: 185 us -> 182 us (0.984)
  Pallas kernels: 182 us -> 179 us
    pallas_call x1, Pallas kernels: 126 us -> 123 us  [block_all(): pl.pallas_call(functools.partial(block_kernel, sizes, layout), out_shape=...]
where the time goes in v6:
time: 182 us; the launch traced here: 181 us
  Pallas kernels  179 us (98%)
    pallas_call x1, Pallas kernels, block_all(): pl.pallas_call(functools.partial(block_kernel, sizes, layout), out_shape=...  123 us
    pallas_call x1, Pallas kernels, attend_all(): pl.pallas_call(functools.partial(attend_kernel, steps), out_shape=[shape(...  51.5 us
    pallas_call x1, Pallas kernels, last_all(): pl.pallas_call(functools.partial(last_kernel, layout), grid=(steps,), out...  4.44 us

profile of v6, /device:TPU:0, one launch (start us, length us, event | category | flops | bytes accessed | tf_op | source)
XLA Modules:
  0.0 181.3 jit_solution(10699143625533204503)
XLA Ops:
  0.7 1.5 convert_add_fusion.vec_ref
  2.2 51.5 %shard_map.305 = (bf16[7,512,768]{2,1,0:T(8,128)(2,1)}, bf16[7,576,512]{2,1,0:T(8,128)(2,1)}, bf16[7,4,192,128]{3,2,1,0:T(8,128)(2,1)}, f32[7,3,512]{2,1,0:T(4,128)}, bf16[7,4,192,128]{3,2,1,0:T(8,128)(2,1)}) custom-call(bf16[7,128,768]{2,1,0:T(8,128)(2,1)} %x_ref.1, s32[7]{0:T(128)} %len_ref.3, bf16[192,768]{1,0:T(8,128)(2,1)} %bitcast.12, ...), custom_call_target="tpu_custom_call" | custom-call | tf_op jit(solution)/shard_map/pallas_call | solution.py:477
  53.7 123.0 %shard_map.306 = (bf16[896,768]{1,0:T(8,128)(2,1)}, f32[896,768]{1,0:T(8,128)}, f32[224,768]{1,0:T(8,128)}, f32[3,32,576]{2,1,0:T(8,128)}, f32[16,768]{1,0:T(8,128)}) custom-call(bf16[896,768]{1,0:T(8,128)(2,1)} %bitcast.10, bf16[7,4,192,128]{3,2,1,0:T(8,128)(2,1)} %get-tuple-element.44.tok_ref, bf16[896,768]{1,0:T(8,128)(2,1)} %bitcast.11, ...), custom_call_target="tpu_custom_call" | custom-call | tf_op jit(solution)/shard_map/pallas_call | solution.py:1004
  176.7 4.4 %shard_map.307 = (bf16[896,768]{1,0:T(8,128)(2,1)}, f32[896,768]{1,0:T(8,128)}, f32[96,192]{1,0:T(8,128)}, f32[96,192]{1,0:T(8,128)}, f32[96,192]{1,0:T(8,128)},...) custom-call(bf16[896,768]{1,0:T(8,128)(2,1)} %get-tuple-element.49.o, ...), custom_call_target="tpu_custom_call" | custom-call | tf_op jit(solution)/shard_map/pallas_call | solution.py:1118

commit v7 on v6

--- a/solution.py
+++ b/solution.py
@@ -303,7 +303,7 @@
 
     def turn(self, t):
         for level in reversed(range(1, len(self.steps))):
-            part = t - 2 * (level - 1)
+            part = t - (2 * (level - 1) - (level == len(self.steps) - 1))
             if isinstance(t, int):
                 if 0 <= part < self.layout.parts:
                     self.land(part, level)
@@ -954,7 +954,7 @@
     far_copy(last).wait_recv()
     branch[last * block :] = branch[last * block :] + far_land[last % 2].astype(F32)
     dx_copy(last).start()
-    last_turn = layout.parts + 2 * (count - 2)
+    last_turn = layout.parts + 2 * (count - 2) - 1
     for t in range(max(last_turn - groups, head.parts + len(dp_steps) - 1, count)):
         wide.turn(t + groups)
         for level in reversed(range(len(dp_steps))):

time: 182 us -> 182 us (level)
  no operation moved by 1% of the time
where the time goes in v7:
time: 182 us; the launch traced here: 181 us
  Pallas kernels  179 us (98%)
    pallas_call x1, Pallas kernels, block_all(): pl.pallas_call(functools.partial(block_kernel, sizes, layout), out_shape=...  123 us
    pallas_call x1, Pallas kernels, attend_all(): pl.pallas_call(functools.partial(attend_kernel, steps), out_shape=[shape(...  51.5 us
    pallas_call x1, Pallas kernels, last_all(): pl.pallas_call(functools.partial(last_kernel, layout), grid=(steps,), out...  4.44 us

profile of v7, /device:TPU:0, one launch (start us, length us, event | category | flops | bytes accessed | tf_op | source)
XLA Modules:
  0.0 181.3 jit_solution(6162502450754802962)
XLA Ops:
  0.7 1.5 convert_add_fusion.vec_ref
  2.2 51.5 %shard_map.305 = (bf16[7,512,768]{2,1,0:T(8,128)(2,1)}, bf16[7,576,512]{2,1,0:T(8,128)(2,1)}, bf16[7,4,192,128]{3,2,1,0:T(8,128)(2,1)}, f32[7,3,512]{2,1,0:T(4,128)}, bf16[7,4,192,128]{3,2,1,0:T(8,128)(2,1)}) custom-call(bf16[7,128,768]{2,1,0:T(8,128)(2,1)} %x_ref.1, s32[7]{0:T(128)} %len_ref.3, bf16[192,768]{1,0:T(8,128)(2,1)} %bitcast.12, ...), custom_call_target="tpu_custom_call" | custom-call | tf_op jit(solution)/shard_map/pallas_call | solution.py:477
  53.7 123.0 %shard_map.306 = (bf16[896,768]{1,0:T(8,128)(2,1)}, f32[896,768]{1,0:T(8,128)}, f32[224,768]{1,0:T(8,128)}, f32[3,32,576]{2,1,0:T(8,128)}, f32[16,768]{1,0:T(8,128)}) custom-call(bf16[896,768]{1,0:T(8,128)(2,1)} %bitcast.10, bf16[7,4,192,128]{3,2,1,0:T(8,128)(2,1)} %get-tuple-element.44.tok_ref, bf16[896,768]{1,0:T(8,128)(2,1)} %bitcast.11, ...), custom_call_target="tpu_custom_call" | custom-call | tf_op jit(solution)/shard_map/pallas_call | solution.py:1004
  176.7 4.4 %shard_map.307 = (bf16[896,768]{1,0:T(8,128)(2,1)}, f32[896,768]{1,0:T(8,128)}, f32[96,192]{1,0:T(8,128)}, f32[96,192]{1,0:T(8,128)}, f32[96,192]{1,0:T(8,128)},...) custom-call(bf16[896,768]{1,0:T(8,128)(2,1)} %get-tuple-element.49.o, ...), custom_call_target="tpu_custom_call" | custom-call | tf_op jit(solution)/shard_map/pallas_call | solution.py:1118
